TPU v7x, 32 devices: a whole 2x2x4 slice. The times are simulated.
32 devices in a mesh: dp: 4 (over z), fsdp: 8 (over y, x, core).
Axes of the slice: x: 2, y: 2, z: 4, core: 2. Of those that a mesh axis runs over, the one named last changes fastest.
Arguments:
- tokens: bfloat16 [32768, 512], P(('dp', 'fsdp')), may hold values from -6 to 6
- chain_ids: int32 [32, 1024], P(('dp', 'fsdp')), may hold values from 0 to 127, as said below
- qkv_weight: bfloat16 [512, 1536], P(('dp', 'fsdp')), may hold values from -0.25 to 0.25
- mix_weight: bfloat16 [512, 512], P(('dp', 'fsdp')), may hold values from -0.75 to 0.75
- up_weight: bfloat16 [512, 2048], P(('dp', 'fsdp')), may hold values from -0.25 to 0.25
- down_weight: bfloat16 [2048, 512], P(('dp', 'fsdp')), may hold values from -0.125 to 0.125
- norm_gain: bfloat16 [2, 512], P(None, ('dp', 'fsdp')), may hold values from 0.5 to 1.5
- norm_bias: bfloat16 [2, 512], P(None, ('dp', 'fsdp')), may hold values from -1.796875 to 1.796875
- qv_bias: bfloat16 [2, 512], P(None, ('dp', 'fsdp')), may hold values from -1.796875 to 1.796875
- proj_bias: bfloat16 [2, 512], P(None, ('dp', 'fsdp')), may hold values from -1.796875 to 1.796875
- up_bias: bfloat16 [2048], P(('dp', 'fsdp')), may hold values from -1.796875 to 1.796875
- cotangent: bfloat16 [32768, 512], P(('dp', 'fsdp')), may hold values from -6 to 6
Outputs:
- output: bfloat16 [32768, 512], P(('dp', 'fsdp'))
- input_grad: float32 [32768, 512], P(('dp', 'fsdp'))
- qkv_grad: float32 [512, 1536], P(('dp', 'fsdp'))
- mix_grad: float32 [512, 512], P(('dp', 'fsdp'))
- up_grad: float32 [512, 2048], P(('dp', 'fsdp'))
- down_grad: float32 [2048, 512], P(('dp', 'fsdp'))
- norm_gain_grad: float32 [2, 512], P(None, ('dp', 'fsdp'))
- norm_bias_grad: float32 [2, 512], P(None, ('dp', 'fsdp'))
- qv_bias_grad: float32 [2, 512], P(None, ('dp', 'fsdp'))
- proj_bias_grad: float32 [2, 512], P(None, ('dp', 'fsdp'))
- up_bias_grad: float32 [2048], P(('dp', 'fsdp'))
Inputs may be any that keep to these rules, and one draw needn't show every extreme that they name: `chain_ids`: in each row (the residues of one device) the chain numbers start at 0 and never fall; residues with one number form one chain, and a new chain begins only at a position that is a multiple of 8. In every draw some device holds a single chain of all 1024 residues.
All inputs are finite; a program needn't handle non-finite values.
Results may differ from a plain program's by a relative error of at most 0.0093.
Values may be sent and summed in bfloat16 or wider, within the bound.
No kernel may reach another device: no remote copies, remote signals or barrier semaphores. Data moves between devices by JAX's collectives and lax.ppermute only.
A program may use at most 256 MiB of HBM per device.

v0:
```python
import jax
import jax.numpy as jnp
from jax import lax
from jax.sharding import PartitionSpec as P

HEADS = 8


NEG = -1e30
EPS = 1e-05


def normalize(rows_in, gain_row, shift_row):
    row_mean = jnp.mean(rows_in, axis=-1, keepdims=True)
    centred = rows_in - row_mean
    spread = jnp.mean(centred * centred, axis=-1, keepdims=True)
    return centred * lax.rsqrt(spread + EPS) * gain_row + shift_row


def gelu_exact(pre_act):
    return jax.nn.gelu(pre_act, approximate=False)


def fetch(
    qkv_weight,
    mix_weight,
    up_weight,
    down_weight,
    norm_gain,
    norm_bias,
    qv_bias,
    proj_bias,
    up_bias,
):
    gathered = (
        lax.all_gather(qkv_weight, ("dp", "fsdp"), axis=0, tiled=True),
        lax.all_gather(mix_weight, ("dp", "fsdp"), axis=0, tiled=True),
        lax.all_gather(up_weight, ("dp", "fsdp"), axis=0, tiled=True),
        lax.all_gather(down_weight, ("dp", "fsdp"), axis=0, tiled=True),
        lax.all_gather(norm_gain, ("dp", "fsdp"), axis=1, tiled=True),
        lax.all_gather(norm_bias, ("dp", "fsdp"), axis=1, tiled=True),
        lax.all_gather(qv_bias, ("dp", "fsdp"), axis=1, tiled=True),
        lax.all_gather(proj_bias, ("dp", "fsdp"), axis=1, tiled=True),
        lax.all_gather(up_bias, ("dp", "fsdp"), axis=0, tiled=True),
    )
    return gathered


def reduce_terms(
    qkv_term,
    mix_term,
    up_term,
    down_term,
    gain_terms,
    shift_terms,
    qv_terms,
    proj_terms,
    up_bias_term,
):
    summed = (
        lax.psum_scatter(qkv_term, ("dp", "fsdp"), scatter_dimension=0, tiled=True),
        lax.psum_scatter(mix_term, ("dp", "fsdp"), scatter_dimension=0, tiled=True),
        lax.psum_scatter(up_term, ("dp", "fsdp"), scatter_dimension=0, tiled=True),
        lax.psum_scatter(down_term, ("dp", "fsdp"), scatter_dimension=0, tiled=True),
        lax.psum_scatter(gain_terms, ("dp", "fsdp"), scatter_dimension=1, tiled=True),
        lax.psum_scatter(shift_terms, ("dp", "fsdp"), scatter_dimension=1, tiled=True),
        lax.psum_scatter(qv_terms, ("dp", "fsdp"), scatter_dimension=1, tiled=True),
        lax.psum_scatter(proj_terms, ("dp", "fsdp"), scatter_dimension=1, tiled=True),
        lax.psum_scatter(up_bias_term, ("dp", "fsdp"), scatter_dimension=0, tiled=True),
    )
    return summed


def body(
    tokens,
    chain_ids,
    qkv_weight,
    mix_weight,
    up_weight,
    down_weight,
    norm_gain,
    norm_bias,
    qv_bias,
    proj_bias,
    up_bias,
    cotangent,
):
    row_count = tokens.shape[0]
    model_width = tokens.shape[1]
    head_count = HEADS
    head_size = model_width // head_count
    block_rows = min(512, row_count)
    chains = chain_ids[0]
    gathered = fetch(
        qkv_weight,
        mix_weight,
        up_weight,
        down_weight,
        norm_gain,
        norm_bias,
        qv_bias,
        proj_bias,
        up_bias,
    )
    gains = gathered[4].astype(jnp.float32)
    shifts = gathered[5].astype(jnp.float32)
    qv_full = gathered[6].astype(jnp.float32)
    proj_full = gathered[7].astype(jnp.float32)
    up_full = gathered[8].astype(jnp.float32)
    stream = tokens.astype(jnp.float32)
    normed, first_back = jax.vjp(normalize, stream, gains[0], shifts[0])
    normed_low = normed.astype(jnp.bfloat16)
    mixed_rows = jnp.dot(normed_low, gathered[0], preferred_element_type=jnp.float32)
    queries = (
        (mixed_rows[:, :model_width] + qv_full[0])
        .astype(jnp.bfloat16)
        .reshape(row_count, head_count, head_size)
    )
    key_rows = (
        mixed_rows[:, model_width : 2 * model_width]
        .astype(jnp.bfloat16)
        .reshape(row_count, head_count, head_size)
    )
    values = (
        (mixed_rows[:, 2 * model_width :] + qv_full[1])
        .astype(jnp.bfloat16)
        .reshape(row_count, head_count, head_size)
    )
    attended_parts = []
    lse_parts = []
    for offset in range(0, row_count, block_rows):
        query_block = queries[offset : offset + block_rows]
        scores = (
            jnp.einsum("qhe,khe->hqk", query_block, key_rows, preferred_element_type=jnp.float32)
            * 0.125
        )
        allowed = (chains[offset : offset + block_rows, None] == chains[None, :])[None]
        masked = jnp.where(allowed, scores, NEG)
        row_peak = jnp.max(masked, axis=-1, keepdims=True)
        row_total = jnp.sum(jnp.exp(masked - row_peak), axis=-1, keepdims=True)
        log_total = row_peak + jnp.log(row_total)
        attn_probs = jnp.where(allowed, jnp.exp(masked - log_total), 0.0).astype(jnp.bfloat16)
        block_out = jnp.einsum(
            "hqk,khe->qhe", attn_probs, values, preferred_element_type=jnp.float32
        )
        attended_parts.append(block_out.reshape(block_rows, model_width))
        lse_parts.append(log_total)
    attended = jnp.concatenate(attended_parts, axis=0).astype(jnp.bfloat16)
    middle = (
        stream + jnp.dot(attended, gathered[1], preferred_element_type=jnp.float32) + proj_full[0]
    )
    normed_two, second_back = jax.vjp(normalize, middle, gains[1], shifts[1])
    normed_two_low = normed_two.astype(jnp.bfloat16)
    pre_act = jnp.dot(normed_two_low, gathered[2], preferred_element_type=jnp.float32) + up_full
    activated, gelu_back = jax.vjp(gelu_exact, pre_act)
    act_low = activated.astype(jnp.bfloat16)
    result = (
        middle + jnp.dot(act_low, gathered[3], preferred_element_type=jnp.float32) + proj_full[1]
    )
    output = result.astype(jnp.bfloat16)
    weights = fetch(
        qkv_weight,
        mix_weight,
        up_weight,
        down_weight,
        norm_gain,
        norm_bias,
        qv_bias,
        proj_bias,
        up_bias,
    )
    grad_out = cotangent.astype(jnp.float32)
    down_term = jnp.einsum("tf,td->fd", act_low, cotangent, preferred_element_type=jnp.float32)
    out_bias_term = jnp.sum(grad_out, axis=0)
    grad_act = jnp.einsum("td,fd->tf", cotangent, weights[3], preferred_element_type=jnp.float32)
    (grad_pre,) = gelu_back(grad_act)
    pre_low = grad_pre.astype(jnp.bfloat16)
    up_term = jnp.einsum("td,tf->df", normed_two_low, pre_low, preferred_element_type=jnp.float32)
    up_bias_term = jnp.sum(pre_low.astype(jnp.float32), axis=0)
    grad_norm_two = jnp.einsum("tf,df->td", pre_low, weights[2], preferred_element_type=jnp.float32)
    grad_middle_norm, gain_two_term, shift_two_term = second_back(grad_norm_two)
    grad_middle = grad_out + grad_middle_norm
    branch_low = grad_middle.astype(jnp.bfloat16)
    mix_term = jnp.einsum("td,te->de", attended, branch_low, preferred_element_type=jnp.float32)
    mix_bias_term = jnp.sum(branch_low.astype(jnp.float32), axis=0)
    grad_attended = jnp.einsum(
        "te,de->td", branch_low, weights[1], preferred_element_type=jnp.float32
    )
    grad_attended = grad_attended.astype(jnp.bfloat16).reshape(row_count, head_count, head_size)
    grad_keys = jnp.zeros((row_count, head_count, head_size), jnp.float32)
    grad_values = jnp.zeros((row_count, head_count, head_size), jnp.float32)
    grad_query_parts = []
    for block_index, offset in enumerate(range(0, row_count, block_rows)):
        query_block = queries[offset : offset + block_rows]
        scores = (
            jnp.einsum("qhe,khe->hqk", query_block, key_rows, preferred_element_type=jnp.float32)
            * 0.125
        )
        allowed = (chains[offset : offset + block_rows, None] == chains[None, :])[None]
        masked = jnp.where(allowed, scores, NEG)
        probs_full = jnp.where(allowed, jnp.exp(masked - lse_parts[block_index]), 0.0)
        grad_block = grad_attended[offset : offset + block_rows]
        grad_probs = jnp.einsum(
            "qhe,khe->hqk", grad_block, values, preferred_element_type=jnp.float32
        )
        row_inner = jnp.sum(probs_full * grad_probs, axis=-1, keepdims=True)
        grad_scores = (probs_full * (grad_probs - row_inner)).astype(jnp.bfloat16)
        grad_query_parts.append(
            jnp.einsum("hqk,khe->qhe", grad_scores, key_rows, preferred_element_type=jnp.float32)
            * 0.125
        )
        grad_keys = (
            grad_keys
            + jnp.einsum(
                "hqk,qhe->khe", grad_scores, query_block, preferred_element_type=jnp.float32
            )
            * 0.125
        )
        grad_values = grad_values + jnp.einsum(
            "hqk,qhe->khe",
            probs_full.astype(jnp.bfloat16),
            grad_block,
            preferred_element_type=jnp.float32,
        )
    grad_queries = jnp.concatenate(grad_query_parts, axis=0)
    grad_mixed = jnp.concatenate(
        [
            grad_queries.reshape(row_count, model_width),
            grad_keys.reshape(row_count, model_width),
            grad_values.reshape(row_count, model_width),
        ],
        axis=1,
    ).astype(jnp.bfloat16)
    qkv_term = jnp.einsum("td,te->de", normed_low, grad_mixed, preferred_element_type=jnp.float32)
    mixed_sums = jnp.sum(grad_mixed.astype(jnp.float32), axis=0)
    qv_terms = jnp.stack([mixed_sums[:model_width], mixed_sums[2 * model_width :]])
    grad_norm_one = jnp.einsum(
        "te,de->td", grad_mixed, weights[0], preferred_element_type=jnp.float32
    )
    grad_stream_norm, gain_one_term, shift_one_term = first_back(grad_norm_one)
    input_grad = grad_middle + grad_stream_norm
    summed = reduce_terms(
        qkv_term,
        mix_term,
        up_term,
        down_term,
        jnp.stack([gain_one_term, gain_two_term]),
        jnp.stack([shift_one_term, shift_two_term]),
        qv_terms,
        jnp.stack([mix_bias_term, out_bias_term]),
        up_bias_term,
    )
    return (
        output,
        input_grad,
        summed[0],
        summed[1],
        summed[2],
        summed[3],
        summed[4],
        summed[5],
        summed[6],
        summed[7],
        summed[8],
    )


def solution(mesh):
    return jax.shard_map(
        body,
        mesh=mesh,
        in_specs=(
            P(("dp", "fsdp"), None),
            P(("dp", "fsdp"), None),
            P(("dp", "fsdp"), None),
            P(("dp", "fsdp"), None),
            P(("dp", "fsdp"), None),
            P(("dp", "fsdp"), None),
            P(None, ("dp", "fsdp")),
            P(None, ("dp", "fsdp")),
            P(None, ("dp", "fsdp")),
            P(None, ("dp", "fsdp")),
            P(("dp", "fsdp")),
            P(("dp", "fsdp"), None),
        ),
        out_specs=(
            P(("dp", "fsdp"), None),
            P(("dp", "fsdp"), None),
            P(("dp", "fsdp"), None),
            P(("dp", "fsdp"), None),
            P(("dp", "fsdp"), None),
            P(("dp", "fsdp"), None),
            P(None, ("dp", "fsdp")),
            P(None, ("dp", "fsdp")),
            P(None, ("dp", "fsdp")),
            P(None, ("dp", "fsdp")),
            P(("dp", "fsdp")),
        ),
        check_vma=False,
    )
```

profile of v0, /device:TPU:0, one launch (start us, length us, event | category | flops | bytes accessed | tf_op | source)
XLA Modules:
  0.0 1507.5 jit_solution(6834171137089755085)
XLA Ops:
  10.3 42.0 %all-reduce = bf16[2048]{0:T(1024)(128)(2,1)S(1)} all-reduce(bf16[2048]{0:T(1024)(128)(2,1)S(1)} %dynamic-update-slice), channel_id=1, replica_groups=mesh['dp'=4,'fsdp'=8] {'dp','fsdp'}, use_global_device_ids=true, to_apply=%add | all-reduce | flops 2048 | bytes 8192
  53.0 40.2 %all-gather = bf16[32,16,2]{1,2,0:T(2,128)(2,1)S(1)} all-gather(bf16[1,16,2]{1,2,0:T(2,128)(2,1)} %bitcast.179), channel_id=1, replica_groups=mesh['dp'=4,'fsdp'=8] {'dp','fsdp'}, dimensions={0}, use_global_device_ids=true | all-gather | bytes 2112 | tf_op jit(solution)/shard_map/all_gather | solution.py:40
  93.3 36.7 %all-gather.1 = bf16[32,16,2]{1,2,0:T(2,128)(2,1)S(1)} all-gather(bf16[1,16,2]{1,2,0:T(2,128)(2,1)} %bitcast.180), channel_id=1, replica_groups=mesh['dp'=4,'fsdp'=8] {'dp','fsdp'}, dimensions={0}, use_global_device_ids=true | all-gather | bytes 2112 | tf_op jit(solution)/shard_map/all_gather | solution.py:41
  130.1 37.8 %all-gather.2 = bf16[32,16,2]{1,2,0:T(2,128)(2,1)S(1)} all-gather(bf16[1,16,2]{1,2,0:T(2,128)(2,1)} %bitcast.181), channel_id=1, replica_groups=mesh['dp'=4,'fsdp'=8] {'dp','fsdp'}, dimensions={0}, use_global_device_ids=true | all-gather | bytes 2112 | tf_op jit(solution)/shard_map/all_gather | solution.py:42
  168.0 36.7 %all-gather.3 = bf16[32,16,2]{1,2,0:T(2,128)(2,1)S(1)} all-gather(bf16[1,16,2]{1,2,0:T(2,128)(2,1)} %bitcast.182), channel_id=1, replica_groups=mesh['dp'=4,'fsdp'=8] {'dp','fsdp'}, dimensions={0}, use_global_device_ids=true | all-gather | bytes 2112 | tf_op jit(solution)/shard_map/all_gather | solution.py:43
  206.2 42.5 %all_gather.35 = bf16[512,512]{1,0:T(8,128)(2,1)} all-gather(bf16[16,512]{1,0:T(8,128)(2,1)} %param.15), channel_id=1, replica_groups=mesh['dp'=4,'fsdp'=8] {'dp','fsdp'}, dimensions={0}, use_global_device_ids=true | all-gather | bytes 540672 | tf_op jit(solution)/shard_map/all_gather | solution.py:37
  291.4 8.3 exponential_reduce_fusion.1
  304.9 8.2 convolution_convert_fusion.2
  314.3 24.6 %multiply_convert_fusion.2 = (bf16[1024,2048]{1,0:T(8,128)(2,1)}, f32[1024,2048]{1,0:T(8,128)}, f32[1024,2048]{1,0:T(8,128)}) fusion(f32[2048]{0:T(1024)S(1)} %convert_element_type.85, bf16[512,2048]{1,0:T(8,128)(2,1)} %all-gather.10.cloned.1.call-done, f32[1024,512]{0,1:T(8,128)S(1)} %get-tuple-element.92, f32[512]{0:T(512)S(1)} %bitcast.172, ...), kind=kOutput, calls=%fused_computation.16 | convolution fusion | flops 2288517120 | bytes 25186304 | tf_op jit(solution)/shard_map/dot_general | solution.py:154
  338.8 10.3 convert_reduce_fusion
  365.1 9.8 fusion.44
  375.0 14.3 multiply_reduce_fusion.1
  389.3 12.0 multiply_reduce_fusion
  401.2 29.5 %multiply_convert_fusion = (bf16[8,512,1024]{2,1,0:T(8,128)(2,1)}, bf16[8,512,1024]{2,1,0:T(8,128)(2,1)}) fusion(f32[8,512,1024]{2,1,0:T(8,128)} %get-tuple-element.97, f32[8,512]{1,0:T(8,128)} %get-tuple-element.96, f32[8,512]{1,0:T(8,128)} %copy-done.32, f32[8,512,1024]{2,1,0:T(8,128)} %copy-done, pred[512,1024]{1,0:T(8,128)(4,1)S(1)} %copy-done.11, ...), kind=kLoop, calls=%fused_computation | loop fusion | flops 58720256 | bytes 85000192 | tf_op jit(solution)/shard_map/convert_element_type | solution.py:207
  438.8 9.0 add_convert_fusion.1
  501.5 37.0 %all-reduce.1 = f32[2048]{0:T(1024)S(1)} all-reduce(f32[2048]{0:T(1024)S(1)} %copy-done.46), channel_id=10, replica_groups=mesh['dp'=4,'fsdp'=8] {'dp','fsdp'}, use_global_device_ids=true, to_apply=%region_30.31.clone | all-reduce | flops 2048 | bytes 16384
  539.1 44.9 %reduce-scatter.29.cloned.1.call-done = f32[16,2]{1,0:T(8,128)} async-done(((f32[512,2]{1,0:T(8,128)}), f32[16,2]{1,0:T(8,128)}) %reduce-scatter.29.cloned.1.call-update) | async-done | bytes 144
  585.3 130.6 %reduce-scatter.27.cloned.1.call-done = f32[16,2]{1,0:T(8,128)} async-done(((f32[512,2]{1,0:T(8,128)}), f32[16,2]{1,0:T(8,128)}) %reduce-scatter.27.cloned.1.call-update) | async-done | bytes 144
  717.3 130.5 %reduce-scatter.31.cloned.1.call-done = f32[16,2]{1,0:T(8,128)} async-done(((f32[512,2]{1,0:T(8,128)}), f32[16,2]{1,0:T(8,128)}) %reduce-scatter.31.cloned.1.call-update) | async-done | bytes 144
  849.2 130.7 %reduce-scatter.25.cloned.1.call-done = f32[16,2]{1,0:T(8,128)} async-done(((f32[512,2]{1,0:T(8,128)}), f32[16,2]{1,0:T(8,128)}) %reduce-scatter.25.cloned.1.call-update) | async-done | bytes 144
  981.2 132.6 %reduce-scatter.19.cloned.1.call-done = f32[16,512]{1,0:T(8,128)} async-done(((f32[512,512]{1,0:T(8,128)}), f32[16,512]{1,0:T(8,128)}) %reduce-scatter.19.cloned.1.call-update) | async-done | bytes 32784 | tf_op jit(solution)/shard_map/reduce_scatter | solution.py:62
  1113.8 104.4 %reduce-scatter.17.cloned.1.call-done = f32[16,1536]{1,0:T(8,128)} async-done(((f32[512,1536]{1,0:T(8,128)}), f32[16,1536]{1,0:T(8,128)}) %reduce-scatter.17.cloned.1.call-update) | async-done | bytes 98320 | tf_op jit(solution)/shard_map/reduce_scatter | solution.py:61
  1218.2 142.5 %reduce-scatter.23.cloned.1.call-done = f32[64,512]{1,0:T(8,128)} async-done(((f32[2048,512]{1,0:T(8,128)}), f32[64,512]{1,0:T(8,128)}) %reduce-scatter.23.cloned.1.call-update) | async-done | bytes 131088 | tf_op jit(solution)/shard_map/reduce_scatter | solution.py:64
  1360.7 139.8 %reduce-scatter.21.cloned.1.call-done = f32[16,2048]{1,0:T(8,128)} async-done(((f32[512,2048]{1,0:T(8,128)}), f32[16,2048]{1,0:T(8,128)}) %reduce-scatter.21.cloned.1.call-update) | async-done | bytes 131088 | tf_op jit(solution)/shard_map/reduce_scatter | solution.py:63
  (243 shorter events, 137.3 us)
Async XLA Ops:
  7.2 247.7 %all-gather.8.cloned.1.call-start = ((), (), s32[]{:S(2)}) async-start(), calls=%async_computation.8 | async-start | bytes 1622016 | tf_op jit(solution)/shard_map/all_gather | solution.py:36
  7.9 306.3 %all-gather.10.cloned.1.call-start = ((), (), s32[]{:S(2)}) async-start(), calls=%async_computation.9 | async-start | bytes 2162688 | tf_op jit(solution)/shard_map/all_gather | solution.py:38
  8.7 330.2 %all-gather.12.cloned.1.call-start = ((), (), s32[]{:S(2)}) async-start(), calls=%async_computation.10 | async-start | bytes 2162688 | tf_op jit(solution)/shard_map/all_gather | solution.py:39
  9.4 574.6 %reduce-scatter.29.cloned.1.call-start = ((), (), s32[]{:S(2)}) async-start(), calls=%async_computation.17 | async-start | bytes 270336
  205.9 52.7 %copy-start.50 = (f32[1,512]{1,0:T(1,128)}, f32[1,512]{1,0:T(1,128)S(1)}, u32[]{:S(2)}) copy-start(f32[1,512]{1,0:T(1,128)S(1)} %get-tuple-element.80) | copy-start | bytes 6148
  205.9 108.3 %copy-start.48 = (f32[1,512]{1,0:T(1,128)}, f32[1,512]{1,0:T(1,128)S(1)}, u32[]{:S(2)}) copy-start(f32[1,512]{1,0:T(1,128)S(1)} %get-tuple-element.79) | copy-start | bytes 6148
  206.1 52.5 %copy-start.40 = (f32[1,512]{1,0:T(1,128)}, f32[1,512]{1,0:T(1,128)S(1)}, u32[]{:S(2)}) copy-start(f32[1,512]{1,0:T(1,128)S(1)} %get-tuple-element.78) | copy-start | bytes 6148
  206.1 153.1 %copy-start.42 = (f32[1,512]{1,0:T(1,128)}, f32[1,512]{1,0:T(1,128)S(1)}, u32[]{:S(2)}) copy-start(f32[1,512]{1,0:T(1,128)S(1)} %get-tuple-element.77) | copy-start | bytes 6148
  250.1 62.9 %copy-start.2 = (bf16[1024,512]{0,1:T(8,128)(2,1)}, bf16[1024,512]{0,1:T(8,128)(2,1)S(1)}, u32[]{:S(2)}) copy-start(bf16[1024,512]{0,1:T(8,128)(2,1)S(1)} %copy.78) | copy-start | bytes 3145732
  254.8 44.9 %copy-start.10 = (pred[512,1024]{1,0:T(8,128)(4,1)}, pred[512,1024]{1,0:T(8,128)(4,1)S(1)}, u32[]{:S(2)}) copy-start(pred[512,1024]{1,0:T(8,128)(4,1)S(1)} %get-tuple-element.82) | copy-start | bytes 1572868
  254.9 50.0 %copy-start.12 = (pred[512,1024]{1,0:T(8,128)(4,1)}, pred[512,1024]{1,0:T(8,128)(4,1)S(1)}, u32[]{:S(2)}) copy-start(pred[512,1024]{1,0:T(8,128)(4,1)S(1)} %get-tuple-element.81) | copy-start | bytes 1572868
  279.6 20.2 %copy-start = (f32[8,512,1024]{2,1,0:T(8,128)}, f32[8,512,1024]{2,1,0:T(8,128)S(1)}, u32[]{:S(2)}) copy-start(f32[8,512,1024]{2,1,0:T(8,128)S(1)} %get-tuple-element.88) | copy-start | bytes 50331652
  313.9 45.4 %copy-start.7 = (f32[1024,512]{0,1:T(8,128)}, f32[1024,512]{0,1:T(8,128)S(1)}, u32[]{:S(2)}) copy-start(f32[1024,512]{0,1:T(8,128)S(1)} %get-tuple-element.92) | copy-start | bytes 6291460
  314.2 24.6 %copy-start.23 = (bf16[1024,512]{1,0:T(8,128)(2,1)S(1)}, bf16[1024,512]{1,0:T(8,128)(2,1)}, u32[]{:S(2)}) copy-start(bf16[1024,512]{1,0:T(8,128)(2,1)} %param.23) | copy-start | bytes 3145732
  365.1 24.1 %slice-start = ((s8[16777216]{0:T(1024)(128)(4,1)}), s8[4194304]{0:T(1024)(128)(4,1)S(1)}, s32[]{:S(2)}) async-start(s8[16777216]{0:T(1024)(128)(4,1)} %bitcast.110), calls=%async_computation.19 | async-start | bytes 8388608
  365.1 24.1 %slice-start.1 = ((s8[16777216]{0:T(1024)(128)(4,1)}), s8[4194304]{0:T(1024)(128)(4,1)S(1)}, s32[]{:S(2)}) async-start(s8[16777216]{0:T(1024)(128)(4,1)} %bitcast.110), calls=%async_computation.20 | async-start | bytes 8388608
  401.2 29.5 %copy-start.5 = (bf16[1024,512]{0,1:T(8,128)(2,1)S(1)}, bf16[1024,512]{0,1:T(8,128)(2,1)}, u32[]{:S(2)}) copy-start(bf16[1024,512]{0,1:T(8,128)(2,1)} %copy-done.4) | copy-start | bytes 3145732
  453.8 262.2 %reduce-scatter.27.cloned.1.call-start = ((), (), s32[]{:S(2)}) async-start(), calls=%async_computation.16 | async-start | bytes 270336
  467.4 380.4 %reduce-scatter.31.cloned.1.call-start = ((), (), s32[]{:S(2)}) async-start(), calls=%async_computation.18 | async-start | bytes 270336
  468.3 511.6 %reduce-scatter.25.cloned.1.call-start = ((), (), s32[]{:S(2)}) async-start(), calls=%async_computation.15 | async-start | bytes 270336
  469.3 644.5 %reduce-scatter.19.cloned.1.call-start = ((), (), s32[]{:S(2)}) async-start(), calls=%async_computation.12 | async-start | bytes 1081344 | tf_op jit(solution)/shard_map/reduce_scatter | solution.py:62
  472.7 745.5 %reduce-scatter.17.cloned.1.call-start = ((), (), s32[]{:S(2)}) async-start(), calls=%async_computation.11 | async-start | bytes 3244032 | tf_op jit(solution)/shard_map/reduce_scatter | solution.py:61
  478.5 882.2 %reduce-scatter.23.cloned.1.call-start = ((), (), s32[]{:S(2)}) async-start(), calls=%async_computation.14 | async-start | bytes 4325376 | tf_op jit(solution)/shard_map/reduce_scatter | solution.py:64
  485.3 1015.2 %reduce-scatter.21.cloned.1.call-start = ((), (), s32[]{:S(2)}) async-start(), calls=%async_computation.13 | async-start | bytes 4325376 | tf_op jit(solution)/shard_map/reduce_scatter | solution.py:63
  (51 other events, 356.8 us)
Sparse Core Ops, SparseCore 0:
  10.9 57.6 all-gather.7
  71.4 55.3 all-gather.9
  129.7 55.2 all-gather.11
  453.8 130.1 reduce-scatter.28
  586.2 129.7 reduce-scatter.26
  718.0 129.7 reduce-scatter.30
  850.1 129.7 reduce-scatter.24
  982.7 131.0 reduce-scatter.18
  1120.7 97.4 reduce-scatter.16
  1221.0 139.6 reduce-scatter.22
  1363.6 136.8 reduce-scatter.20
where the time goes:
time: 1510 us
  waiting for transfers between devices  958 us (63%)
  blocking collectives  273 us (18%)
  matrix products  158 us (10%)
  other arithmetic  61.1 us (4%)
  local copies, waits for them, and re-layouts  40.7 us (3%)
  between operations  15.4 us (1%)
    unnamed x15, waiting for transfers between devices  439 us
    reduce_scatter x1, waiting for transfers between devices, reduce_terms(): lax.psum_scatter(down_term, ('dp', 'fsdp'), scatter_dimension=0, tiled=True)  142 us
    reduce_scatter x1, waiting for transfers between devices, reduce_terms(): lax.psum_scatter(up_term, ('dp', 'fsdp'), scatter_dimension=0, tiled=True)  140 us
    reduce_scatter x1, waiting for transfers between devices, reduce_terms(): lax.psum_scatter(mix_term, ('dp', 'fsdp'), scatter_dimension=0, tiled=True)  133 us
    reduce_scatter x1, waiting for transfers between devices, reduce_terms(): lax.psum_scatter(qkv_term, ('dp', 'fsdp'), scatter_dimension=0, tiled=True)  104 us
    unnamed x2, blocking collectives  79 us
    all_gather x1, blocking collectives, fetch(): lax.all_gather(mix_weight, ('dp', 'fsdp'), axis=0, tiled=True)  42.5 us
    all_gather x1, blocking collectives, fetch(): lax.all_gather(norm_gain, ('dp', 'fsdp'), axis=1, tiled=True)  40.2 us
  transfers between devices with their start and end apart: 11, of which 8 were waited for; matrix products, arithmetic and copies ran while one was open for 9% of the time, Pallas kernels for 0%

commit v1 on v0

v1 whole, which is shorter than its diff:
```python
import math

import jax
import jax.numpy as jnp
from jax import lax
from jax.experimental import pallas as pl
from jax.experimental.pallas import tpu as pltpu
from jax.sharding import PartitionSpec as P

AXES = ("dp", "fsdp")
HEADS = 8
EPS = 1e-05
SCALE = 0.125
EXP_SCALE = SCALE * math.log2(math.e)
HIDE = -(2.0**60)
MIB = 2**20

BF = jnp.bfloat16
F32 = jnp.float32
NN = (((1,), (0,)), ((), ()))
NT = (((1,), (1,)), ((), ()))
TN = (((0,), (0,)), ((), ()))


def dot(a, b, dims=NN):
    return lax.dot_general(a, b, dims, preferred_element_type=F32)


def vmem():
    return pl.BlockSpec(memory_space=pltpu.VMEM)


def smem():
    return pl.BlockSpec(memory_space=pltpu.SMEM)


def shape(dims, dtype):
    return jax.ShapeDtypeStruct(dims, dtype)


def slots():
    return [(c, j, i) for c in range(2) for j in range(4) for i in range(4)]


def block_row(me, c, j, i, rows):
    return pl.multiple_of((me ^ (c | (j << 1) | (i << 3))) * rows, rows)


def row_stats(rows_in):
    mean = jnp.mean(rows_in, axis=-1, keepdims=True)
    centred = rows_in - mean
    spread = jnp.mean(centred * centred, axis=-1, keepdims=True)
    return centred, lax.rsqrt(spread + EPS)


def split_three(row):
    first = row.astype(BF).astype(F32)
    rest = row - first
    second = rest.astype(BF).astype(F32)
    return first, second, rest - second


def pack_kernel(qkv, mix, up, down, gain, shift, qv, proj, up_bias, a0, a1, b0, b1, rows128):
    for pair in range(4):
        target, base = (a0, a1)[pair // 2], (pair % 2) * 384
        for part in range(3):
            target[:, base + 128 * part : base + 128 * part + 128] = qkv[
                :, 512 * part + 128 * pair : 512 * part + 128 * pair + 128
            ]
    rows128[...] = jnp.zeros_like(rows128)
    for index, ref in enumerate((gain, shift, qv, proj)):
        rows128[2 * index : 2 * index + 2, :] = ref[...].astype(F32)
    eye = (
        lax.broadcasted_iota(jnp.int32, (16, 16), 0) == lax.broadcasted_iota(jnp.int32, (16, 16), 1)
    ).astype(F32)
    columns = dot(eye.astype(BF), rows128[...].astype(BF), NT)
    bias = jnp.concatenate([jnp.zeros((1, 64), F32), up_bias[...].astype(F32)], axis=1)
    row = lax.broadcasted_iota(jnp.int32, (16, 128), 0)
    lane = lax.broadcasted_iota(jnp.int32, (16, 128), 1)
    a0[:, 768:896] = jnp.where((row == 0) & (lane >= 64), bias, columns).astype(BF)
    b0[:, 0:512] = mix[...]
    b0[:, 512:2560] = up[...]
    for part in range(4):
        b1[:, 512 * part : 512 * part + 512] = down[16 * part : 16 * part + 16, :]


def pack(qkv, mix, up, down, gain, shift, qv, proj, up_bias):
    return pl.pallas_call(
        pack_kernel,
        in_specs=[vmem()] * 9,
        out_specs=[vmem()] * 4,
        out_shape=[
            shape((16, 896), BF),
            shape((16, 768), BF),
            shape((16, 2560), BF),
            shape((16, 2048), BF),
        ],
        scratch_shapes=[pltpu.VMEM((128, 16), F32)],
        name="pack",
    )(qkv, mix, up, down, gain, shift, qv, proj, up_bias.reshape(1, 64))


def aux_rows(chain):
    row = lax.broadcasted_iota(jnp.int32, (128, chain.shape[1]), 0)
    low_bits = jnp.where(row < 7, (chain >> jnp.minimum(row, 6)) & 1, 0)
    high_bits = jnp.where(
        (row >= 7) & (row < 14), 1 - ((chain >> jnp.minimum(jnp.maximum(row - 7, 0), 6)) & 1), 0
    )
    bits = low_bits + high_bits
    query_side = bits.astype(F32) * HIDE
    key_side = jnp.where(row < 14, 1 - bits, jnp.where(row < 17, 1, 0)).astype(F32)
    return query_side.astype(BF), key_side.T.astype(BF)


def pair_forward(normed, weight, bias_q, bias_v, key_aux, qa, ot, outs, pair, block):
    q_out, k_out, v_out, o_out, ot_out, lse_out = outs
    rows = normed.shape[0]
    cols = slice(128 * pair, 128 * pair + 128)
    q2 = (dot(normed, weight[:, 0:128]) + bias_q).astype(BF)
    k2 = dot(normed, weight[:, 128:256]).astype(BF)
    v2 = (dot(normed, weight[:, 256:384]) + bias_v).astype(BF)
    q_out[:, cols] = q2
    k_out[:, cols] = k2
    v_out[:, cols] = v2
    qa[0:128, :] = q2.T
    vt = v2.T
    ones = (lax.broadcasted_iota(jnp.int32, (16, rows), 0) == 0).astype(F32).astype(BF)
    lane = lax.broadcasted_iota(jnp.int32, k2.shape, 1)
    zero = jnp.zeros_like(k2)
    keys = [
        jnp.concatenate([jnp.where((lane >= 64) == bool(h), k2, zero), key_aux], axis=1)
        for h in range(2)
    ]
    vts = [jnp.concatenate([vt[64 * h : 64 * h + 64], ones], axis=0) for h in range(2)]
    count = rows // block

    def score(index):
        q_cols = qa[:, block * index : block * index + block]
        return [dot(keys[h], q_cols) for h in range(2)]

    ahead = score(0)
    for index in range(count):
        scores = ahead
        if index + 1 < count:
            ahead = score(index + 1)
        span = slice(block * index, block * index + block)
        for h in range(2):
            peak = jnp.max(scores[h], axis=0, keepdims=True)
            probs = jnp.exp2((scores[h] - peak) * EXP_SCALE).astype(BF)
            mixed = dot(vts[h], probs)
            total = mixed[64:65]
            ot[64 * h : 64 * h + 64, span] = mixed[:64] * (1.0 / total)
            lse_out[2 * pair + h : 2 * pair + h + 1, span] = peak + jnp.log(total) * (1.0 / SCALE)
    ot_out[128 * pair : 128 * pair + 128, :] = ot[...].astype(BF)
    o_out[:, cols] = ot[...].T.astype(BF)


def assemble(me, mine, other, target, width):
    for c, j, i in slots():
        source = (mine, other)[c]
        target[pl.ds(block_row(me, c, j, i, 16), 16), :] = source[4 * j + i, :, 0:width]


def forward_first_kernel(
    me_ref, tokens, chain, mine, other,
    q_out, k_out, v_out, o_out, ot_out, lse_out, weight, normed_out, normed_t, smalls, up_row,
    key_aux_out, query_aux_out, qa, ot, columns,
):
    me = me_ref[0]
    assemble(me, mine, other, weight, 768)
    for c, j, i in slots():
        source = (mine, other)[c]
        columns[pl.ds(block_row(me, c, j, i, 16), 16), :] = source[4 * j + i, :, 768:896].astype(F32)
    smalls[...] = columns[...].T[0:8, :]
    lane = lax.broadcasted_iota(jnp.int32, (1, 128), 1)
    for a in range(16):
        even = pltpu.roll(columns[32 * a : 32 * a + 8, :], 64, 1)[0:1, :]
        odd = columns[32 * a + 16 : 32 * a + 17, :]
        up_row[:, 128 * a : 128 * a + 128] = jnp.where(lane < 64, even, odd)
    query_side, key_side = aux_rows(chain[...])
    qa[128:256, :] = query_side
    query_aux_out[...] = query_side
    key_aux_out[...] = key_side

    def norm_block(index, carry):
        span = pl.ds(pl.multiple_of(index * 256, 256), 256)
        centred, scale = row_stats(tokens[span, :].astype(F32))
        normed_out[span, :] = (centred * scale * smalls[0:1, :] + smalls[2:3, :]).astype(BF)
        return carry

    lax.fori_loop(0, tokens.shape[0] // 256, norm_block, 0)
    normed = normed_out[...]
    normed_t[0:512, :] = normed.T
    ones_row = lax.broadcasted_iota(jnp.int32, (16, normed.shape[0]), 0) == 0
    normed_t[512:528, :] = ones_row.astype(F32).astype(BF)
    outs = (q_out, k_out, v_out, o_out, ot_out, lse_out)
    for pair in range(2):
        cols = slice(128 * pair, 128 * pair + 128)
        pair_forward(
            normed, weight[:, 384 * pair : 384 * pair + 384], smalls[4:5, cols], smalls[5:6, cols],
            key_side, qa, ot, outs, pair, 512,
        )


def forward_second_kernel(
    me_ref, normed_in, mine, other, smalls, key_aux, query_aux,
    q_out, k_out, v_out, o_out, ot_out, lse_out, weight, qa, ot,
):
    me = me_ref[0]
    assemble(me, mine, other, weight, 768)
    qa[128:256, :] = query_aux[...]
    normed = normed_in[...]
    outs = (q_out, k_out, v_out, o_out, ot_out, lse_out)
    for pair in range(2):
        cols = slice(256 + 128 * pair, 256 + 128 * pair + 128)
        pair_forward(
            normed, weight[:, 384 * pair : 384 * pair + 384], smalls[4:5, cols], smalls[5:6, cols],
            key_aux[...], qa, ot, outs, pair, 512,
        )


def forward_shapes(rows):
    return [shape((rows, 256), BF)] * 4 + [
        shape((256, rows), BF),
        shape((4, rows), F32),
        shape((512, 768), BF),
    ]


def forward_scratch(rows):
    return [pltpu.VMEM((256, rows), BF), pltpu.VMEM((128, rows), F32)]


def forward_first(me, tokens, chain, mine, other):
    rows = tokens.shape[0]
    return pl.pallas_call(
        forward_first_kernel,
        in_specs=[smem()] + [vmem()] * 4,
        out_specs=[vmem()] * 13,
        out_shape=forward_shapes(rows)
        + [
            shape((rows, 512), BF),
            shape((528, rows), BF),
            shape((8, 512), F32),
            shape((1, 2048), F32),
            shape((rows, 128), BF),
            shape((128, rows), BF),
        ],
        scratch_shapes=forward_scratch(rows) + [pltpu.VMEM((512, 128), F32)],
        compiler_params=pltpu.CompilerParams(vmem_limit_bytes=40 * MIB),
        name="attend_first",
    )(me, tokens, chain, mine, other)


def forward_second(me, normed, mine, other, smalls, key_aux, query_aux):
    rows = normed.shape[0]
    return pl.pallas_call(
        forward_second_kernel,
        in_specs=[smem()] + [vmem()] * 6,
        out_specs=[vmem()] * 7,
        out_shape=forward_shapes(rows),
        scratch_shapes=forward_scratch(rows),
        compiler_params=pltpu.CompilerParams(vmem_limit_bytes=40 * MIB),
        name="attend_second",
    )(me, normed, mine, other, smalls, key_aux, query_aux)


def gelu_parts(u):
    half_cdf = 0.5 + 0.5 * lax.erf(u * math.sqrt(0.5))
    density = jnp.exp2(u * u * (-0.5 * math.log2(math.e))) * (1.0 / math.sqrt(2.0 * math.pi))
    return u * half_cdf, half_cdf + u * density


def scatter_blocks(me, source, rows, base_block, blocks, send, keep, span):
    core = me & 1
    for half in range(blocks // 2):
        first = base_block + 2 * half
        row = 2 * half * rows
        r = (me ^ first) >> 1
        place = ((r & 3) << 2) | (r >> 2)
        kept = source[pl.ds(pl.multiple_of(row + core * rows, rows), rows), :]
        sent = source[pl.ds(pl.multiple_of(row + (1 - core) * rows, rows), rows), :]
        keep[place, :, span] = kept
        send[place, :, span] = sent.astype(BF)


def feed_kernel(
    me_ref, tokens, o_first, o_second, ot_first, ot_second, mine_a, other_a, mine_b, other_b,
    smalls, up_row, cot,
    output, grad_middle, grad_att, d_send, d_keep, u_send, u_keep, m_send, m_keep, small_grads,
    up_bias_grad, mix, up, down, middle, normed, normed_t, total, back, stage_d, stage_u, stats,
):
    me = me_ref[0]
    for c, j, i in slots():
        first, second = ((mine_a, mine_b), (other_a, other_b))[c]
        row = block_row(me, c, j, i, 16)
        mix[pl.ds(row, 16), :] = first[4 * j + i, :, 0:512]
        up[pl.ds(row, 16), :] = first[4 * j + i, :, 512:2560]
        for part in range(4):
            row4 = pl.multiple_of(block_row(me, c, j, i, 64) + 16 * part, 16)
            down[pl.ds(row4, 16), :] = second[4 * j + i, :, 512 * part : 512 * part + 512]
    rows = tokens.shape[0]
    block = 256
    count = rows // block

    def ahead(index, carry):
        span = pl.ds(pl.multiple_of(index * block, block), block)
        att = jnp.concatenate([o_first[span, :], o_second[span, :]], axis=1)
        mid = tokens[span, :].astype(F32) + dot(att, mix[...]) + smalls[6:7, :]
        middle[span, :] = mid
        centred, scale = row_stats(mid)
        normed[span, :] = (centred * scale * smalls[1:2, :] + smalls[3:4, :]).astype(BF)
        total[span, :] = mid + smalls[7:8, :]
        return carry

    lax.fori_loop(0, count, ahead, 0)
    back[...] = jnp.zeros_like(back)
    normed_t[0:512, :] = normed[...].T
    ones_row = lax.broadcasted_iota(jnp.int32, (16, rows), 0) == 0
    normed_t[512:528, :] = ones_row.astype(F32).astype(BF)

    width = 512
    for chunk in range(2048 // width):
        span = slice(chunk * width, chunk * width + width)
        up_part = up[:, span]
        down_part = down[span, :]
        act_parts = []
        pre = dot(normed[...], up_part) + up_row[:, span]
        act, slope = gelu_parts(pre)
        act_low = act.astype(BF)
        grad_pre = (dot(cot[...], down_part, NT) * slope).astype(BF)
        total[...] += dot(act_low, down_part)
        stage_d[...] = dot(act_low, cot[...], TN)
        back[...] += dot(grad_pre, up_part, NT)
        stage_u[...] = dot(normed_t[...], grad_pre)
        up_bias_grad[:, span] = stage_u[512:513, :]
        scatter_blocks(me, stage_d, 64, chunk * width // 64, width // 64, d_send, d_keep, slice(None))
        scatter_blocks(me, stage_u, 16, 0, 32, u_send, u_keep, span)
    output[...] = total[...].astype(BF)

    def behind(index, carry):
        gain_sum, shift_sum, branch_sum, cot_sum = carry
        span = pl.ds(pl.multiple_of(index * block, block), block)
        centred, scale = row_stats(middle[span, :])
        xh = centred * scale
        h = back[span, :]
        hg = h * smalls[1:2, :]
        cot_rows = cot[span, :].astype(F32)
        grad = cot_rows + scale * (
            hg
            - jnp.mean(hg, axis=-1, keepdims=True)
            - xh * jnp.mean(hg * xh, axis=-1, keepdims=True)
        )
        grad_middle[span, :] = grad
        low = grad.astype(BF)
        normed[span, :] = low
        grad_att[span, :] = dot(low, mix[...], NT).astype(BF)
        return (
            gain_sum + jnp.sum(h * xh, axis=0, keepdims=True),
            shift_sum + jnp.sum(h, axis=0, keepdims=True),
            branch_sum + jnp.sum(low.astype(F32), axis=0, keepdims=True),
            cot_sum + jnp.sum(cot_rows, axis=0, keepdims=True),
        )

    zero = jnp.zeros((1, 512), F32)
    sums = lax.fori_loop(0, count, behind, (zero, zero, zero, zero))
    for index in range(4):
        small_grads[index : index + 1, :] = sums[index]
    small_grads[4:8, :] = jnp.zeros((4, 512), F32)
    stage_d[0:256, :] = dot(ot_first[...], normed[...])
    stage_d[256:512, :] = dot(ot_second[...], normed[...])
    scatter_blocks(me, stage_d, 16, 0, 32, m_send, m_keep, slice(None))


def feed(me, tokens, o_pair, ot_pair, a_pair, b_pair, smalls, up_row, cot):
    rows = tokens.shape[0]
    return pl.pallas_call(
        feed_kernel,
        in_specs=[smem()] + [vmem()] * 12,
        out_specs=[vmem()] * 11,
        out_shape=[
            shape((rows, 512), BF),
            shape((rows, 512), F32),
            shape((rows, 512), BF),
            shape((16, 64, 512), BF),
            shape((16, 64, 512), F32),
            shape((16, 16, 2048), BF),
            shape((16, 16, 2048), F32),
            shape((16, 16, 512), BF),
            shape((16, 16, 512), F32),
            shape((8, 512), F32),
            shape((1, 2048), F32),
        ],
        scratch_shapes=[
            pltpu.VMEM((512, 512), BF),
            pltpu.VMEM((512, 2048), BF),
            pltpu.VMEM((2048, 512), BF),
            pltpu.VMEM((rows, 512), F32),
            pltpu.VMEM((rows, 512), BF),
            pltpu.VMEM((528, rows), BF),
            pltpu.VMEM((rows, 512), F32),
            pltpu.VMEM((rows, 512), F32),
            pltpu.VMEM((512, 512), F32),
            pltpu.VMEM((528, 512), F32),
            pltpu.VMEM((8, 128), F32),
        ],
        compiler_params=pltpu.CompilerParams(vmem_limit_bytes=56 * MIB),
        name="feed",
    )(me, tokens, *o_pair, *ot_pair, *a_pair, *b_pair, smalls, up_row, cot)


def pair_backward(q, k, v, do, ot_in, lse, key_aux, qa, da, dqt, acc_k, acc_v, gm, pair, block):
    cols = slice(128 * pair, 128 * pair + 128)
    k2 = k[:, cols]
    v2 = v[:, cols]
    rows = k2.shape[0]
    kt = k2.T
    lane = lax.broadcasted_iota(jnp.int32, k2.shape, 1)
    zero = jnp.zeros_like(k2)
    keys = []
    vals = []
    for h in range(2):
        own = (lane >= 64) == bool(h)
        keys.append(jnp.concatenate([jnp.where(own, k2, zero), key_aux], axis=1))
        vals.append(jnp.concatenate([jnp.where(own, v2, zero), key_aux], axis=1))
    qt = q[:, cols].T
    dt = do[:, cols].T
    product = dt.astype(F32) * ot_in[cols, :].astype(F32)
    row = lax.broadcasted_iota(jnp.int32, (16, rows), 0)
    for h in range(2):
        qa[h, 0:128, :] = qt
        da[h, 0:128, :] = dt
        delta = jnp.sum(product[64 * h : 64 * h + 64], axis=0, keepdims=True)
        base = qa[h, 128:144, :].astype(F32)
        one, two, three = split_three(-lse[2 * pair + h : 2 * pair + h + 1, :])
        base = jnp.where(row == 14, one, jnp.where(row == 15, two, base))
        qa[h, 128:144, :] = base.astype(BF)
        qa[h, 144:160, :] = jnp.where(row == 0, three, 0.0).astype(BF)
        one, two, three = split_three(-delta)
        base = jnp.where(row == 14, one, jnp.where(row == 15, two, 0.0))
        da[h, 128:144, :] = base.astype(BF)
        da[h, 144:160, :] = jnp.where(row == 0, three, 0.0).astype(BF)
    small_lane = lax.broadcasted_iota(jnp.int32, (block, 128), 1)
    for index in range(rows // block):
        span = slice(block * index, block * index + block)
        do_rows = do[span, cols]
        q_rows = q[span, cols]
        blank = jnp.zeros_like(do_rows)
        sum_k = None
        sum_v = None
        for h in range(2):
            own = (small_lane >= 64) == bool(h)
            probs = jnp.exp2(dot(keys[h], qa[h, :, span]) * EXP_SCALE)
            grad = (probs * dot(vals[h], da[h, :, span])).astype(BF)
            probs = probs.astype(BF)
            dqt[64 * h : 64 * h + 64, span] = dot(kt[64 * h : 64 * h + 64, :], grad)
            part_k = dot(grad, jnp.where(own, q_rows, blank))
            part_v = dot(probs, jnp.where(own, do_rows, blank))
            sum_k = part_k if sum_k is None else sum_k + part_k
            sum_v = part_v if sum_v is None else sum_v + part_v
        if index == 0:
            acc_k[...] = sum_k
            acc_v[...] = sum_v
        else:
            acc_k[...] += sum_k
            acc_v[...] += sum_v
    base = 384 * pair
    gm[:, base : base + 128] = (dqt[...].T * SCALE).astype(BF)
    gm[:, base + 128 : base + 256] = (acc_k[...] * SCALE).astype(BF)
    gm[:, base + 256 : base + 384] = acc_v[...].astype(BF)


def backward_group(
    me, q, k, v, do, ot_in, lse, key_aux, query_aux, normed_t, q_send, q_keep, sums, scratch
):
    qa, da, dqt, acc_k, acc_v, gm, stage = scratch
    for h in range(2):
        qa[h, 128:256, :] = query_aux[...]
        da[h, 128:256, :] = jnp.zeros((128, da.shape[2]), BF)
    for pair in range(2):
        pair_backward(
            q, k, v, do, ot_in, lse, key_aux[...], qa, da, dqt, acc_k, acc_v, gm, pair, 256
        )
    stage[...] = dot(normed_t[...], gm[...])
    sums[...] = stage[512:520, :]
    scatter_blocks(me, stage, 16, 0, 32, q_send, q_keep, slice(0, 768))


def backward_first_kernel(
    me_ref, q, k, v, do, ot_in, lse, key_aux, query_aux, normed_t, weight,
    q_send, q_keep, sums, partial, *scratch,
):
    backward_group(
        me_ref[0], q, k, v, do, ot_in, lse, key_aux, query_aux, normed_t, q_send, q_keep, sums,
        scratch,
    )
    gm = scratch[5]
    partial[...] = dot(gm[...], weight[...], NT)


def backward_second_kernel(
    me_ref, q, k, v, do, ot_in, lse, key_aux, query_aux, normed_t, weight, partial, tokens,
    smalls, grad_middle, small_grads, up_bias_grad, sums_first,
    q_send, q_keep, input_grad, *scratch,
):
    me = me_ref[0]
    sums, columns = scratch[7], scratch[8]
    backward_group(
        me, q, k, v, do, ot_in, lse, key_aux, query_aux, normed_t, q_send, q_keep, sums,
        scratch[:7],
    )
    gm = scratch[5]
    block = 256

    def behind(index, carry):
        gain_sum, shift_sum = carry
        span = pl.ds(pl.multiple_of(index * block, block), block)
        centred, scale = row_stats(tokens[span, :].astype(F32))
        xh = centred * scale
        h = partial[span, :] + dot(gm[span, :], weight[...], NT)
        hg = h * smalls[0:1, :]
        input_grad[span, :] = grad_middle[span, :] + scale * (
            hg
            - jnp.mean(hg, axis=-1, keepdims=True)
            - xh * jnp.mean(hg * xh, axis=-1, keepdims=True)
        )
        return (
            gain_sum + jnp.sum(h * xh, axis=0, keepdims=True),
            shift_sum + jnp.sum(h, axis=0, keepdims=True),
        )

    zero = jnp.zeros((1, 512), F32)
    gain_sum, shift_sum = lax.fori_loop(0, tokens.shape[0] // block, behind, (zero, zero))
    columns[...] = jnp.zeros_like(columns)
    columns[0:1, :] = gain_sum
    columns[1:2, :] = small_grads[0:1, :]
    columns[2:3, :] = shift_sum
    columns[3:4, :] = small_grads[1:2, :]
    for pair in range(4):
        source = (sums_first, sums)[pair // 2]
        base = (pair % 2) * 384
        span = slice(128 * pair, 128 * pair + 128)
        columns[4:5, span] = source[0:1, base : base + 128]
        columns[5:6, span] = source[0:1, base + 256 : base + 384]
    columns[6:7, :] = small_grads[2:3, :]
    columns[7:8, :] = small_grads[3:4, :]
    stage = scratch[6]
    stage[0:512, 0:128] = columns[...].T
    lane = lax.broadcasted_iota(jnp.int32, (1, 128), 1)
    for a in range(16):
        piece = up_bias_grad[:, 128 * a : 128 * a + 128]
        rolled = pltpu.roll(jnp.broadcast_to(piece, (8, 128)), 64, 1)[0:1, :]
        for half, values in enumerate((rolled, piece)):
            row = 32 * a + 16 * half
            stage[row : row + 1, 0:128] = jnp.where(lane < 64, stage[row : row + 1, 0:128], values)
    core = me & 1
    for half in range(16):
        r = (me ^ (2 * half)) >> 1
        place = ((r & 3) << 2) | (r >> 2)
        kept = pl.multiple_of(32 * half + core * 16, 16)
        sent = pl.multiple_of(32 * half + (1 - core) * 16, 16)
        q_keep[place, :, 768:896] = stage[pl.ds(kept, 16), 0:128]
        q_send[place, :, 768:896] = stage[pl.ds(sent, 16), 0:128].astype(BF)


def backward_scratch(rows):
    return [
        pltpu.VMEM((2, 256, rows), BF),
        pltpu.VMEM((2, 256, rows), BF),
        pltpu.VMEM((128, rows), F32),
        pltpu.VMEM((rows, 128), F32),
        pltpu.VMEM((rows, 128), F32),
        pltpu.VMEM((rows, 768), BF),
        pltpu.VMEM((528, 768), F32),
    ]


def backward_first(me, *operands):
    rows = operands[0].shape[0]
    return pl.pallas_call(
        backward_first_kernel,
        in_specs=[smem(), vmem(), vmem(), vmem(), pl.BlockSpec((rows, 256), lambda i: (0, 0))]
        + [vmem()] * 6,
        grid=(1,),
        out_specs=[vmem()] * 4,
        out_shape=[
            shape((16, 16, 768), BF),
            shape((16, 16, 768), F32),
            shape((8, 768), F32),
            shape((rows, 512), F32),
        ],
        scratch_shapes=backward_scratch(rows),
        compiler_params=pltpu.CompilerParams(vmem_limit_bytes=48 * MIB),
        name="attend_back_first",
    )(me, *operands)


def backward_second(me, *operands):
    rows = operands[0].shape[0]
    return pl.pallas_call(
        backward_second_kernel,
        in_specs=[smem(), vmem(), vmem(), vmem(), pl.BlockSpec((rows, 256), lambda i: (0, 1))]
        + [vmem()] * 13,
        grid=(1,),
        out_specs=[vmem()] * 3,
        out_shape=[
            shape((16, 16, 896), BF),
            shape((16, 16, 896), F32),
            shape((rows, 512), F32),
        ],
        scratch_shapes=backward_scratch(rows)
        + [pltpu.VMEM((8, 768), F32), pltpu.VMEM((128, 512), F32)],
        compiler_params=pltpu.CompilerParams(vmem_limit_bytes=48 * MIB),
        name="attend_back_second",
    )(me, *operands)


def swap(value, mask, count):
    return lax.ppermute(value, AXES, [(d, d ^ mask) for d in range(count)])


def spread(part, count):
    column = jnp.stack([part] + [swap(part, i << 3, count) for i in range(1, 4)])
    plane = jnp.stack([column] + [swap(column, j << 1, count) for j in range(1, 4)])
    mine = plane.reshape((16,) + part.shape)
    return mine, swap(mine, 1, count)


def collect(send, keep, count):
    rows, width = send.shape[1:]
    total = (keep + swap(send, 1, count).astype(F32)).reshape(4, 4, rows, width)
    plane = total[0]
    for j in range(1, 4):
        plane = plane + swap(total[j].astype(BF), j << 1, count).astype(F32)
    own = plane[0]
    for i in range(1, 4):
        own = own + swap(plane[i].astype(BF), i << 3, count).astype(F32)
    return own


def pack_whole(qkv, mix, up, down, gain, shift, qv, proj, up_bias):
    pieces = []
    for pair in range(4):
        for part in range(3):
            base = 512 * part + 128 * pair
            pieces.append(qkv[:, base : base + 128])
    rows = jnp.concatenate([gain, shift, qv, proj], axis=0)
    tile = jnp.pad(rows.T, ((0, 0), (0, 120))).reshape(32, 16, 128)
    tile = tile.at[:, 0, 64:128].set(up_bias.reshape(32, 64))
    a0 = jnp.concatenate([jnp.concatenate(pieces[:6], 1).reshape(32, 16, 768), tile], axis=2)
    a1 = jnp.concatenate(pieces[6:], 1).reshape(32, 16, 768)
    b0 = jnp.concatenate([mix, up], axis=1).reshape(32, 16, 2560)
    b1 = down.reshape(32, 4, 16, 512).swapaxes(1, 2).reshape(32, 16, 2048)
    return a0, a1, b0, b1


def relative_halves(blocks):
    parts = blocks.reshape((4, 4, 2) + blocks.shape[1:])
    parts = parts.transpose((2, 1, 0) + tuple(range(3, parts.ndim)))
    return parts[0].reshape((16,) + blocks.shape[1:]), parts[1].reshape((16,) + blocks.shape[1:])


def whole_blocks(send, keep):
    parts = jnp.stack([keep, send.astype(F32)]).reshape((2, 4, 4) + keep.shape[1:])
    parts = parts.transpose((2, 1, 0) + tuple(range(3, parts.ndim)))
    return parts.reshape((32,) + keep.shape[1:])


def body(cubic, count, tokens, chain_ids, qkv, mix, up, down, gain, shift, qv, proj, up_bias, cot):
    params = (qkv, mix, up, down, gain, shift, qv, proj, up_bias)
    if cubic:
        index = lax.axis_index("dp") * (count // lax.axis_size("dp")) + lax.axis_index("fsdp")
        me = index.astype(jnp.int32).reshape(1)
        parts = pack(*params)
        a0, a1, b0, b1 = [spread(part, count) for part in parts]
    else:
        me = jnp.zeros((1,), jnp.int32)
        dims = (0, 0, 0, 0, 1, 1, 1, 1, 0)
        whole = [
            lax.all_gather(value, AXES, axis=dim, tiled=True)
            for value, dim in zip(params, dims, strict=True)
        ]
        a0, a1, b0, b1 = [relative_halves(part) for part in pack_whole(*whole)]
    q0, k0, v0, o0, ot0, lse0, w0, normed, normed_t, smalls, up_row, key_aux, query_aux = (
        forward_first(me, tokens, chain_ids, *a0)
    )
    q1, k1, v1, o1, ot1, lse1, w1 = forward_second(me, normed, *a1, smalls, key_aux, query_aux)
    (
        output, grad_middle, grad_att, d_send, d_keep, u_send, u_keep, m_send, m_keep,
        small_grads, up_bias_grad,
    ) = feed(me, tokens, (o0, o1), (ot0, ot1), b0, b1, smalls, up_row, cot)
    s0, r0, sums0, partial = backward_first(
        me, q0, k0, v0, grad_att, ot0, lse0, key_aux, query_aux, normed_t, w0
    )
    s1, r1, input_grad = backward_second(
        me, q1, k1, v1, grad_att, ot1, lse1, key_aux, query_aux, normed_t, w1, partial, tokens,
        smalls, grad_middle, small_grads, up_bias_grad, sums0,
    )
    pairs = ((d_send, d_keep), (u_send, u_keep), (m_send, m_keep), (s0, r0), (s1, r1))
    if cubic:
        down_grad, up_grad, mix_grad, first, second = [collect(s, r, count) for s, r in pairs]
        tile = second[:, 768:896]
        vectors = tile[:, 0:8].T
        bias_grad = tile[0, 64:128]
        joined = [first, second[:, :768]]
        qkv_grad = unpack_columns(joined)
    else:
        blocks = [whole_blocks(s, r) for s, r in pairs]
        tiles = blocks[4][:, :, 768:896]
        wholes = (
            blocks[0].reshape(2048, 512),
            blocks[1].reshape(512, 2048),
            blocks[2].reshape(512, 512),
            unpack_columns(
                [blocks[3].reshape(512, 768), blocks[4][:, :, :768].reshape(512, 768)]
            ),
            tiles[:, 0, 64:128].reshape(2048),
        )
        down_grad, up_grad, mix_grad, qkv_grad, bias_grad = [
            lax.psum_scatter(value, AXES, scatter_dimension=0, tiled=True) for value in wholes
        ]
        vectors = lax.psum_scatter(
            tiles[:, :, 0:8].reshape(512, 8).T, AXES, scatter_dimension=1, tiled=True
        )
    return (
        output, input_grad, qkv_grad, mix_grad, up_grad, down_grad,
        vectors[0:2], vectors[2:4], vectors[4:6], vectors[6:8], bias_grad,
    )


def unpack_columns(halves):
    pieces = []
    for part in range(3):
        for pair in range(4):
            base = (pair % 2) * 384 + 128 * part
            pieces.append(halves[pair // 2][:, base : base + 128])
    return jnp.concatenate(pieces, axis=1)


def solution(mesh):
    count = mesh.shape["dp"] * mesh.shape["fsdp"]
    cubic = count == 32

    def entry(*operands):
        return body(cubic, count, *operands)

    rows = P(AXES, None)
    columns = P(None, AXES)
    flat = P(AXES)
    return jax.shard_map(
        entry,
        mesh=mesh,
        in_specs=(rows,) * 6 + (columns,) * 4 + (flat, rows),
        out_specs=(rows,) * 6 + (columns,) * 4 + (flat,),
        check_vma=False,
    )
```

time: 1510 us -> 241 us (0.16)
  waiting for transfers between devices: 958 us -> 59 us
  blocking collectives: 273 us -> 0 us
  matrix products: 158 us -> 0 us
  Pallas kernels: 0 us -> 82.8 us
  starting transfers between devices: 0.7 us -> 75.1 us
  other arithmetic: 61.1 us -> 11.5 us
  local copies, waits for them, and re-layouts: 40.7 us -> 7.72 us
    reduce_scatter x4 -> x0, waiting for transfers between devices: 519 us -> none  [the longest x1 142 us: reduce_terms(): lax.psum_scatter(down_term, ('dp', 'fsdp'), scatter_dimension=0, tiled=True)]
    unnamed x15 -> x0, waiting for transfers between devices: 439 us -> none
    all_gather x5 -> x0, blocking collectives: 194 us -> none  [the longest x1 42.5 us: fetch(): lax.all_gather(mix_weight, ('dp', 'fsdp'), axis=0, tiled=True)]
    dot_general x24 -> x0, matrix products: 158 us -> none  [the longest x2 26.2 us: body(): jnp.einsum('qhe,khe->hqk', grad_block, values, preferred_element_type=jnp...]
    pallas_call x0 -> x6, Pallas kernels: none -> 82.8 us  [the longest x1 28.6 us: feed(): pl.pallas_call(feed_kernel, in_specs=[smem()] + [vmem()] * 12, out_specs=...]
    unnamed x2 -> x0, blocking collectives: 79 us -> none
    ppermute x0 -> x63, starting transfers between devices: none -> 75.1 us  [swap(): return lax.ppermute(value, AXES, [(d, d ^ mask) for d in range(count)])]
    ppermute x0 -> x63, waiting for transfers between devices: none -> 59 us  [swap(): return lax.ppermute(value, AXES, [(d, d ^ mask) for d in range(count)])]
  transfers between devices with their start and end apart: 11 -> 63, of which waited for: 8 -> 31; matrix products, arithmetic and copies ran while one was open for 9% -> 6% of each run, Pallas kernels for 0% -> 22%
where the time goes in v1:
time: 241 us; the launch traced here: 238 us
  Pallas kernels  82.8 us (34%)
  starting transfers between devices  75.1 us (31%)
  waiting for transfers between devices  59 us (24%)
  other arithmetic  11.5 us (5%)
  local copies, waits for them, and re-layouts  7.72 us (3%)
    ppermute x63, starting transfers between devices, swap(): return lax.ppermute(value, AXES, [(d, d ^ mask) for d in range(count)])  75.1 us
    ppermute x63, waiting for transfers between devices, swap(): return lax.ppermute(value, AXES, [(d, d ^ mask) for d in range(count)])  59 us
    pallas_call x1, Pallas kernels, feed(): pl.pallas_call(feed_kernel, in_specs=[smem()] + [vmem()] * 12, out_specs=...  28.6 us
    pallas_call x1, Pallas kernels, backward_second(): pl.pallas_call(backward_second_kernel, in_specs=[smem(), vmem(), vmem(),...  20.2 us
    pallas_call x1, Pallas kernels, backward_first(): pl.pallas_call(backward_first_kernel, in_specs=[smem(), vmem(), vmem(), v...  16.8 us
    pallas_call x1, Pallas kernels, forward_first(): pl.pallas_call(forward_first_kernel, in_specs=[smem()] + [vmem()] * 4, ou...  8.6 us
    pallas_call x1, Pallas kernels, forward_second(): pl.pallas_call(forward_second_kernel, in_specs=[smem()] + [vmem()] * 6, o...  6.93 us
    unnamed x55, local copies, waits for them, and re-layouts  6.8 us
  transfers between devices with their start and end apart: 63, of which 31 were waited for; matrix products, arithmetic and copies ran while one was open for 6% of the time, Pallas kernels for 22%

profile of v1, /device:TPU:0, one launch (start us, length us, event | category | flops | bytes accessed | tf_op | source)
XLA Modules:
  0.0 237.6 jit_solution(6516801872093039725)
XLA Ops:
  2.4 5.0 %collective-permute-start.16 = (bf16[16,2560]{1,0:T(8,128)(2,1)}, bf16[16,2560]{1,0:T(8,128)(2,1)S(1)}, u32[]{:S(2)}, u32[]{:S(2)}) collective-permute-start(bf16[16,2560]{1,0:T(8,128)(2,1)} %get-tuple-element.63), channel_id=1, source_target_pairs={{0,24},{1,25},{2,26},{3,27},{4,28},{5,29},{6,30},{7,31},{8,16},{9,... | collective-permute-start | bytes 245768 | tf_op jit(solution)/shard_map/ppermute | solution.py:619
  8.1 3.8 %collective-permute-start.23 = (bf16[16,2048]{1,0:T(8,128)(2,1)}, bf16[16,2048]{1,0:T(8,128)(2,1)S(1)}, u32[]{:S(2)}, u32[]{:S(2)}) collective-permute-start(bf16[16,2048]{1,0:T(8,128)(2,1)} %get-tuple-element.64), channel_id=1, source_target_pairs={{0,24},{1,25},{2,26},{3,27},{4,28},{5,29},{6,30},{7,31},{8,16},{9,... | collective-permute-start | bytes 196616 | tf_op jit(solution)/shard_map/ppermute | solution.py:619
  11.8 4.8 %collective-permute-done.15 = bf16[16,2560]{1,0:T(8,128)(2,1)S(1)} collective-permute-done((bf16[16,2560]{1,0:T(8,128)(2,1)}, bf16[16,2560]{1,0:T(8,128)(2,1)S(1)}, u32[]{:S(2)}, u32[]{:S(2)}) %collective-permute-start.15) | collective-permute-done | bytes 81952 | tf_op jit(solution)/shard_map/ppermute | solution.py:619
  21.1 3.2 %collective-permute-start.21 = (bf16[16,2048]{1,0:T(8,128)(2,1)}, bf16[16,2048]{1,0:T(8,128)(2,1)S(1)}, u32[]{:S(2)}, u32[]{:S(2)}) collective-permute-start(bf16[16,2048]{1,0:T(8,128)(2,1)} %get-tuple-element.64), channel_id=1, source_target_pairs={{0,8},{1,9},{2,10},{3,11},{4,12},{5,13},{6,14},{7,15},{8,0},{9,1},... | collective-permute-start | bytes 196616 | tf_op jit(solution)/shard_map/ppermute | solution.py:619
  24.4 2.7 %collective-permute-done.22 = bf16[16,2048]{1,0:T(8,128)(2,1)S(1)} collective-permute-done((bf16[16,2048]{1,0:T(8,128)(2,1)}, bf16[16,2048]{1,0:T(8,128)(2,1)S(1)}, u32[]{:S(2)}, u32[]{:S(2)}) %collective-permute-start.22) | collective-permute-done | bytes 65568 | tf_op jit(solution)/shard_map/ppermute | solution.py:619
  32.0 4.8 %collective-permute-done.19 = bf16[4,16,2560]{2,1,0:T(8,128)(2,1)S(1)} collective-permute-done((bf16[4,16,2560]{2,1,0:T(8,128)(2,1)S(1)}, bf16[4,16,2560]{2,1,0:T(8,128)(2,1)S(1)}, u32[]{:S(2)}, u32[]{:S(2)}) %collective-permute-start.19) | collective-permute-done | bytes 327712 | tf_op jit(solution)/shard_map/ppermute | solution.py:619
  42.0 2.6 %collective-permute-done.26 = bf16[4,16,2048]{2,1,0:T(8,128)(2,1)S(1)} collective-permute-done((bf16[4,16,2048]{2,1,0:T(8,128)(2,1)S(1)}, bf16[4,16,2048]{2,1,0:T(8,128)(2,1)S(1)}, u32[]{:S(2)}, u32[]{:S(2)}) %collective-permute-start.26) | collective-permute-done | bytes 262176 | tf_op jit(solution)/shard_map/ppermute | solution.py:619
  47.1 3.0 %collective-permute-start = (bf16[16,896]{1,0:T(8,128)(2,1)S(1)}, bf16[16,896]{1,0:T(8,128)(2,1)S(1)}, u32[]{:S(2)}, u32[]{:S(2)}) collective-permute-start(bf16[16,896]{1,0:T(8,128)(2,1)S(1)} %copy-done.17), channel_id=1, source_target_pairs={{0,8},{1,9},{2,10},{3,11},{4,12},{5,13},{6,14},{7,15},{8,0},{9,1},... | collective-permute-start | bytes 86024 | tf_op jit(solution)/shard_map/ppermute | solution.py:619
  52.9 3.1 %collective-permute-start.7 = (bf16[16,768]{1,0:T(8,128)(2,1)S(1)}, bf16[16,768]{1,0:T(8,128)(2,1)S(1)}, u32[]{:S(2)}, u32[]{:S(2)}) collective-permute-start(bf16[16,768]{1,0:T(8,128)(2,1)S(1)} %copy-done.18), channel_id=1, source_target_pairs={{0,8},{1,9},{2,10},{3,11},{4,12},{5,13},{6,14},{7,15},{8,0},{9,1},... | collective-permute-start | bytes 73736 | tf_op jit(solution)/shard_map/ppermute | solution.py:619
  61.0 3.0 %collective-permute-done.4 = bf16[4,16,896]{2,1,0:T(8,128)(2,1)S(1)} collective-permute-done((bf16[4,16,896]{2,1,0:T(8,128)(2,1)S(1)}, bf16[4,16,896]{2,1,0:T(8,128)(2,1)S(1)}, u32[]{:S(2)}, u32[]{:S(2)}) %collective-permute-start.4) | collective-permute-done | bytes 114720 | tf_op jit(solution)/shard_map/ppermute | solution.py:619
  66.9 2.5 %collective-permute-start.12 = (bf16[4,16,768]{2,1,0:T(8,128)(2,1)S(1)}, bf16[4,16,768]{2,1,0:T(8,128)(2,1)S(1)}, u32[]{:S(2)}, u32[]{:S(2)}) collective-permute-start(bf16[4,16,768]{2,1,0:T(8,128)(2,1)S(1)} %get-tuple-element.160), channel_id=1, source_target_pairs={{0,6},{1,7},{2,4},{3,5},{4,2},{5,3},{6,0},{7,1},{8,14},{9,15},{10,... | collective-permute-start | bytes 294920 | tf_op jit(solution)/shard_map/ppermute | solution.py:619
  72.6 8.6 %attend_first.1 = (bf16[1024,256]{1,0:T(8,128)(2,1)S(1)}, bf16[1024,256]{1,0:T(8,128)(2,1)S(1)}, bf16[1024,256]{1,0:T(8,128)(2,1)S(1)}, bf16[1024,256]{1,0:T(8,1...) custom-call(s32[1]{0:T(128)} %bitcast.me_ref, ...), custom_call_target="tpu_custom_call" | custom-call | tf_op jit(solution)/shard_map/attend_first/pallas_call | solution.py:236
  83.8 6.9 %attend_second.1 = (bf16[1024,256]{1,0:T(8,128)(2,1)S(1)}, bf16[1024,256]{1,0:T(8,128)(2,1)S(1)}, bf16[1024,256]{1,0:T(8,128)(2,1)S(1)}, bf16[1024,256]{1,0:T(8,...) custom-call(s32[1]{0:T(128)} %bitcast.me_ref, ...), custom_call_target="tpu_custom_call" | custom-call | tf_op jit(solution)/shard_map/attend_second/pallas_call | solution.py:257
  92.4 28.6 %feed.1 = (bf16[1024,512]{1,0:T(8,128)(2,1)}, f32[1024,512]{1,0:T(8,128)}, bf16[1024,512]{1,0:T(8,128)(2,1)}, bf16[16,64,512]{2,1,0:T(8,128)(2,1)}, f32[16,64,51...) custom-call(s32[1]{0:T(128)} %bitcast.me_ref, ...), custom_call_target="tpu_custom_call" | custom-call | tf_op jit(solution)/shard_map/feed/pallas_call | solution.py:377
  127.7 16.8 %attend_back_first.1 = (bf16[16,16,768]{2,1,0:T(8,128)(2,1)S(1)}, f32[16,16,768]{2,1,0:T(8,128)S(1)}, f32[8,768]{1,0:T(8,128)S(1)}, f32[1024,512]{1,0:T(8,128)}) custom-call(s32[1]{0:T(128)} %bitcast.me_ref, bf16[1024,256]{1,0:T(8,128)(2,1)S(1)} %get-tuple-element.74.q, bf16[1024,256]{1,0:T(8,128)(2,1)S(1)} %get-tuple-element.75.k, ...), custom_call_target="tpu_custom_call" | custom-call | tf_op jit(solution)/shard_map/attend_back_first/pallas_call | solution.py:580
  148.1 20.2 %attend_back_second.1 = (bf16[16,16,896]{2,1,0:T(8,128)(2,1)S(1)}, f32[16,16,896]{2,1,0:T(8,128)S(1)}, f32[1024,512]{1,0:T(8,128)}) custom-call(s32[1]{0:T(128)} %bitcast.me_ref, bf16[1024,256]{1,0:T(8,128)(2,1)S(1)} %get-tuple-element.67.q, bf16[1024,256]{1,0:T(8,128)(2,1)S(1)} %get-tuple-element.68.k, bf16[1024,256]{1,0:T(8,128)(2,1)S(1)} %get-tuple-element.69.v, ...), custom_call_target="tpu_custom_call" | custom-call | tf_op jit(solution)/shard_map/attend_back_second/pallas_call | solution.py:600
  174.9 3.1 %collective-permute-done.31 = bf16[4,16,768]{2,1,0:T(8,128)(2,1)S(1)} collective-permute-done((bf16[4,16,768]{2,1,0:T(8,128)(2,1)S(1)}, bf16[4,16,768]{2,1,0:T(8,128)(2,1)S(1)}, u32[]{:S(2)}, u32[]{:S(2)}) %collective-permute-start.31) | collective-permute-done | bytes 98336 | tf_op jit(solution)/shard_map/ppermute | solution.py:619
  189.2 2.6 %collective-permute-done.38 = bf16[4,16,896]{2,1,0:T(8,128)(2,1)S(1)} collective-permute-done((bf16[4,16,896]{2,1,0:T(8,128)(2,1)S(1)}, bf16[4,16,896]{2,1,0:T(8,128)(2,1)S(1)}, u32[]{:S(2)}, u32[]{:S(2)}) %collective-permute-start.38) | collective-permute-done | bytes 114720 | tf_op jit(solution)/shard_map/ppermute | solution.py:619
  194.6 2.1 collective-permute-start.40
  197.0 2.3 collective-permute-done.41
  215.1 5.2 %collective-permute-done.52 = bf16[4,16,2048]{2,1,0:T(8,128)(2,1)S(1)} collective-permute-done((bf16[4,16,2048]{2,1,0:T(8,128)(2,1)S(1)}, bf16[4,16,2048]{2,1,0:T(8,128)(2,1)S(1)}, u32[]{:S(2)}, u32[]{:S(2)}) %collective-permute-start.52) | collective-permute-done | bytes 262176 | tf_op jit(solution)/shard_map/ppermute | solution.py:619
  222.8 2.6 %collective-permute-start.55 = (bf16[16,2048]{1,0:T(8,128)(2,1)S(1)}, bf16[16,2048]{1,0:T(8,128)(2,1)S(1)}, u32[]{:S(2)}, u32[]{:S(2)}) collective-permute-start(bf16[16,2048]{1,0:T(8,128)(2,1)S(1)} %get-tuple-element.144), channel_id=1, source_target_pairs={{0,24},{1,25},{2,26},{3,27},{4,28},{5,29},{6,30},{7,31},{8,16},{9,... | collective-permute-start | bytes 196616 | tf_op jit(solution)/shard_map/ppermute | solution.py:619
  228.5 2.6 %collective-permute-start.62 = (bf16[64,512]{1,0:T(8,128)(2,1)S(1)}, bf16[64,512]{1,0:T(8,128)(2,1)S(1)}, u32[]{:S(2)}, u32[]{:S(2)}) collective-permute-start(bf16[64,512]{1,0:T(8,128)(2,1)S(1)} %get-tuple-element.141), channel_id=1, source_target_pairs={{0,24},{1,25},{2,26},{3,27},{4,28},{5,29},{6,30},{7,31},{8,16},{9,... | collective-permute-start | bytes 196616 | tf_op jit(solution)/shard_map/ppermute | solution.py:619
  234.6 2.0 collective-permute-done.61
  (200 shorter events, 94.1 us)
Async XLA Ops:
  8.1 13.1 %collective-permute-start.23 = (bf16[16,2048]{1,0:T(8,128)(2,1)}, bf16[16,2048]{1,0:T(8,128)(2,1)S(1)}, u32[]{:S(2)}, u32[]{:S(2)}) collective-permute-start(bf16[16,2048]{1,0:T(8,128)(2,1)} %get-tuple-element.64), channel_id=1, source_target_pairs={{0,24},{1,25},{2,26},{3,27},{4,28},{5,29},{6,30},{7,31},{8,16},{9,... | collective-permute-start | bytes 196616 | tf_op jit(solution)/shard_map/ppermute | solution.py:619
  17.6 13.9 %collective-permute-start.18 = (bf16[4,16,2560]{2,1,0:T(8,128)(2,1)S(1)}, bf16[4,16,2560]{2,1,0:T(8,128)(2,1)S(1)}, u32[]{:S(2)}, u32[]{:S(2)}) collective-permute-start(bf16[4,16,2560]{2,1,0:T(8,128)(2,1)S(1)} %get-tuple-element.139), channel_id=1, source_target_pairs={{0,4},{1,5},{2,6},{3,7},{4,0},{5,1},{6,2},{7,3},{8,12},{9,13},{10,... | collective-permute-start | bytes 983048 | tf_op jit(solution)/shard_map/ppermute | solution.py:619
  19.1 12.9 %collective-permute-start.17 = (bf16[4,16,2560]{2,1,0:T(8,128)(2,1)S(1)}, bf16[4,16,2560]{2,1,0:T(8,128)(2,1)S(1)}, u32[]{:S(2)}, u32[]{:S(2)}) collective-permute-start(bf16[4,16,2560]{2,1,0:T(8,128)(2,1)S(1)} %get-tuple-element.139), channel_id=1, source_target_pairs={{0,2},{1,3},{2,0},{3,1},{4,6},{5,7},{6,4},{7,5},{8,10},{9,11},{10,... | collective-permute-start | bytes 983048 | tf_op jit(solution)/shard_map/ppermute | solution.py:619
  20.6 16.2 %collective-permute-start.19 = (bf16[4,16,2560]{2,1,0:T(8,128)(2,1)S(1)}, bf16[4,16,2560]{2,1,0:T(8,128)(2,1)S(1)}, u32[]{:S(2)}, u32[]{:S(2)}) collective-permute-start(bf16[4,16,2560]{2,1,0:T(8,128)(2,1)S(1)} %get-tuple-element.139), channel_id=1, source_target_pairs={{0,6},{1,7},{2,4},{3,5},{4,2},{5,3},{6,0},{7,1},{8,14},{9,15},{10,... | collective-permute-start | bytes 983048 | tf_op jit(solution)/shard_map/ppermute | solution.py:619
  28.4 11.6 %collective-permute-start.25 = (bf16[4,16,2048]{2,1,0:T(8,128)(2,1)S(1)}, bf16[4,16,2048]{2,1,0:T(8,128)(2,1)S(1)}, u32[]{:S(2)}, u32[]{:S(2)}) collective-permute-start(bf16[4,16,2048]{2,1,0:T(8,128)(2,1)S(1)} %get-tuple-element.150), channel_id=1, source_target_pairs={{0,4},{1,5},{2,6},{3,7},{4,0},{5,1},{6,2},{7,3},{8,12},{9,13},{10,... | collective-permute-start | bytes 786440 | tf_op jit(solution)/shard_map/ppermute | solution.py:619
  30.0 12.0 %collective-permute-start.24 = (bf16[4,16,2048]{2,1,0:T(8,128)(2,1)S(1)}, bf16[4,16,2048]{2,1,0:T(8,128)(2,1)S(1)}, u32[]{:S(2)}, u32[]{:S(2)}) collective-permute-start(bf16[4,16,2048]{2,1,0:T(8,128)(2,1)S(1)} %get-tuple-element.150), channel_id=1, source_target_pairs={{0,2},{1,3},{2,0},{3,1},{4,6},{5,7},{6,4},{7,5},{8,10},{9,11},{10,... | collective-permute-start | bytes 786440 | tf_op jit(solution)/shard_map/ppermute | solution.py:619
  31.5 13.1 %collective-permute-start.26 = (bf16[4,16,2048]{2,1,0:T(8,128)(2,1)S(1)}, bf16[4,16,2048]{2,1,0:T(8,128)(2,1)S(1)}, u32[]{:S(2)}, u32[]{:S(2)}) collective-permute-start(bf16[4,16,2048]{2,1,0:T(8,128)(2,1)S(1)} %get-tuple-element.150), channel_id=1, source_target_pairs={{0,6},{1,7},{2,4},{3,5},{4,2},{5,3},{6,0},{7,1},{8,14},{9,15},{10,... | collective-permute-start | bytes 786440 | tf_op jit(solution)/shard_map/ppermute | solution.py:619
  38.0 54.3 %collective-permute-start.20 = (bf16[16,16,2560]{2,1,0:T(8,128)(2,1)}, bf16[16,16,2560]{2,1,0:T(8,128)(2,1)}, u32[]{:S(2)}, u32[]{:S(2)}) collective-permute-start(bf16[16,16,2560]{2,1,0:T(8,128)(2,1)} %bitcast.28.mine_a), channel_id=1, source_target_pairs={{0,1},{1,0},{2,3},{3,2},{4,5},{5,4},{6,7},{7,6},{8,9},{9,8},{10,11... | collective-permute-start | bytes 3932168 | tf_op jit(solution)/shard_map/ppermute | solution.py:619
  45.7 46.7 %collective-permute-start.27 = (bf16[16,16,2048]{2,1,0:T(8,128)(2,1)}, bf16[16,16,2048]{2,1,0:T(8,128)(2,1)}, u32[]{:S(2)}, u32[]{:S(2)}) collective-permute-start(bf16[16,16,2048]{2,1,0:T(8,128)(2,1)} %bitcast.37.mine_b), channel_id=1, source_target_pairs={{0,1},{1,0},{2,3},{3,2},{4,5},{5,4},{6,7},{7,6},{8,9},{9,8},{10,11... | collective-permute-start | bytes 3145736 | tf_op jit(solution)/shard_map/ppermute | solution.py:619
  72.5 11.3 %collective-permute-start.13 = (bf16[16,16,768]{2,1,0:T(8,128)(2,1)S(1)}, bf16[16,16,768]{2,1,0:T(8,128)(2,1)S(1)}, u32[]{:S(2)}, u32[]{:S(2)}) collective-permute-start(bf16[16,16,768]{2,1,0:T(8,128)(2,1)S(1)} %bitcast.118), channel_id=1, source_target_pairs={{0,1},{1,0},{2,3},{3,2},{4,5},{5,4},{6,7},{7,6},{8,9},{9,8},{10,11... | collective-permute-start | bytes 1179656 | tf_op jit(solution)/shard_map/ppermute | solution.py:619
  124.1 20.4 %collective-permute-start.43 = (bf16[4,16,512]{2,1,0:T(8,128)(2,1)S(1)}, bf16[4,16,512]{2,1,0:T(8,128)(2,1)S(1)}, u32[]{:S(2)}, u32[]{:S(2)}) collective-permute-start(bf16[4,16,512]{2,1,0:T(8,128)(2,1)S(1)} %get-tuple-element.146), channel_id=1, source_target_pairs={{0,2},{1,3},{2,0},{3,1},{4,6},{5,7},{6,4},{7,5},{8,10},{9,11},{10,... | collective-permute-start | bytes 196616 | tf_op jit(solution)/shard_map/ppermute | solution.py:619
  125.2 19.3 %collective-permute-start.45 = (bf16[4,16,512]{2,1,0:T(8,128)(2,1)S(1)}, bf16[4,16,512]{2,1,0:T(8,128)(2,1)S(1)}, u32[]{:S(2)}, u32[]{:S(2)}) collective-permute-start(bf16[4,16,512]{2,1,0:T(8,128)(2,1)S(1)} %get-tuple-element.147), channel_id=1, source_target_pairs={{0,6},{1,7},{2,4},{3,5},{4,2},{5,3},{6,0},{7,1},{8,14},{9,15},{10,... | collective-permute-start | bytes 196616 | tf_op jit(solution)/shard_map/ppermute | solution.py:619
  127.1 17.4 %collective-permute-start.44 = (bf16[4,16,512]{2,1,0:T(8,128)(2,1)S(1)}, bf16[4,16,512]{2,1,0:T(8,128)(2,1)S(1)}, u32[]{:S(2)}, u32[]{:S(2)}) collective-permute-start(bf16[4,16,512]{2,1,0:T(8,128)(2,1)S(1)} %get-tuple-element.148), channel_id=1, source_target_pairs={{0,4},{1,5},{2,6},{3,7},{4,0},{5,1},{6,2},{7,3},{8,12},{9,13},{10,... | collective-permute-start | bytes 196616 | tf_op jit(solution)/shard_map/ppermute | solution.py:619
  144.5 25.0 %collective-permute-start.28 = (bf16[16,16,768]{2,1,0:T(8,128)(2,1)S(1)}, bf16[16,16,768]{2,1,0:T(8,128)(2,1)S(1)}, u32[]{:S(2)}, u32[]{:S(2)}) collective-permute-start(bf16[16,16,768]{2,1,0:T(8,128)(2,1)S(1)} %get-tuple-element.86), channel_id=1, source_target_pairs={{0,1},{1,0},{2,3},{3,2},{4,5},{5,4},{6,7},{7,6},{8,9},{9,8},{10,11... | collective-permute-start | bytes 1179656 | tf_op jit(solution)/shard_map/ppermute | solution.py:619
  144.6 23.7 %collective-permute-start.46 = (bf16[16,512]{1,0:T(8,128)(2,1)S(1)}, bf16[16,512]{1,0:T(8,128)(2,1)S(1)}, u32[]{:S(2)}, u32[]{:S(2)}) collective-permute-start(bf16[16,512]{1,0:T(8,128)(2,1)S(1)} %get-tuple-element.161), channel_id=1, source_target_pairs={{0,8},{1,9},{2,10},{3,11},{4,12},{5,13},{6,14},{7,15},{8,0},{9,1},... | collective-permute-start | bytes 49160 | tf_op jit(solution)/shard_map/ppermute | solution.py:619
  145.2 23.6 %collective-permute-start.48 = (bf16[16,512]{1,0:T(8,128)(2,1)S(1)}, bf16[16,512]{1,0:T(8,128)(2,1)S(1)}, u32[]{:S(2)}, u32[]{:S(2)}) collective-permute-start(bf16[16,512]{1,0:T(8,128)(2,1)S(1)} %get-tuple-element.162), channel_id=1, source_target_pairs={{0,24},{1,25},{2,26},{3,27},{4,28},{5,29},{6,30},{7,31},{8,16},{9,... | collective-permute-start | bytes 49160 | tf_op jit(solution)/shard_map/ppermute | solution.py:619
  146.7 22.1 %collective-permute-start.47 = (bf16[16,512]{1,0:T(8,128)(2,1)S(1)}, bf16[16,512]{1,0:T(8,128)(2,1)S(1)}, u32[]{:S(2)}, u32[]{:S(2)}) collective-permute-start(bf16[16,512]{1,0:T(8,128)(2,1)S(1)} %get-tuple-element.163), channel_id=1, source_target_pairs={{0,16},{1,17},{2,18},{3,19},{4,20},{5,21},{6,22},{7,23},{8,24},{9,... | collective-permute-start | bytes 49160 | tf_op jit(solution)/shard_map/ppermute | solution.py:619
  168.3 34.9 %collective-permute-start.49 = (bf16[16,16,2048]{2,1,0:T(8,128)(2,1)}, bf16[16,16,2048]{2,1,0:T(8,128)(2,1)}, u32[]{:S(2)}, u32[]{:S(2)}) collective-permute-start(bf16[16,16,2048]{2,1,0:T(8,128)(2,1)} %get-tuple-element.92), channel_id=1, source_target_pairs={{0,1},{1,0},{2,3},{3,2},{4,5},{5,4},{6,7},{7,6},{8,9},{9,8},{10,11... | collective-permute-start | bytes 3145736 | tf_op jit(solution)/shard_map/ppermute | solution.py:619
  168.8 39.8 %collective-permute-start.56 = (bf16[16,64,512]{2,1,0:T(8,128)(2,1)}, bf16[16,64,512]{2,1,0:T(8,128)(2,1)}, u32[]{:S(2)}, u32[]{:S(2)}) collective-permute-start(bf16[16,64,512]{2,1,0:T(8,128)(2,1)} %get-tuple-element.94), channel_id=1, source_target_pairs={{0,1},{1,0},{2,3},{3,2},{4,5},{5,4},{6,7},{7,6},{8,9},{9,8},{10,11... | collective-permute-start | bytes 3145736 | tf_op jit(solution)/shard_map/ppermute | solution.py:619
  206.4 13.9 %collective-permute-start.52 = (bf16[4,16,2048]{2,1,0:T(8,128)(2,1)S(1)}, bf16[4,16,2048]{2,1,0:T(8,128)(2,1)S(1)}, u32[]{:S(2)}, u32[]{:S(2)}) collective-permute-start(bf16[4,16,2048]{2,1,0:T(8,128)(2,1)S(1)} %get-tuple-element.130), channel_id=1, source_target_pairs={{0,6},{1,7},{2,4},{3,5},{4,2},{5,3},{6,0},{7,1},{8,14},{9,15},{10,... | collective-permute-start | bytes 786440 | tf_op jit(solution)/shard_map/ppermute | solution.py:619
  207.4 14.9 %collective-permute-start.51 = (bf16[4,16,2048]{2,1,0:T(8,128)(2,1)S(1)}, bf16[4,16,2048]{2,1,0:T(8,128)(2,1)S(1)}, u32[]{:S(2)}, u32[]{:S(2)}) collective-permute-start(bf16[4,16,2048]{2,1,0:T(8,128)(2,1)S(1)} %get-tuple-element.131), channel_id=1, source_target_pairs={{0,4},{1,5},{2,6},{3,7},{4,0},{5,1},{6,2},{7,3},{8,12},{9,13},{10,... | collective-permute-start | bytes 786440 | tf_op jit(solution)/shard_map/ppermute | solution.py:619
  210.4 15.0 %collective-permute-start.57 = (bf16[4,64,512]{2,1,0:T(8,128)(2,1)S(1)}, bf16[4,64,512]{2,1,0:T(8,128)(2,1)S(1)}, u32[]{:S(2)}, u32[]{:S(2)}) collective-permute-start(bf16[4,64,512]{2,1,0:T(8,128)(2,1)S(1)} %get-tuple-element.126), channel_id=1, source_target_pairs={{0,2},{1,3},{2,0},{3,1},{4,6},{5,7},{6,4},{7,5},{8,10},{9,11},{10,... | collective-permute-start | bytes 786440 | tf_op jit(solution)/shard_map/ppermute | solution.py:619
  211.7 15.0 %collective-permute-start.59 = (bf16[4,64,512]{2,1,0:T(8,128)(2,1)S(1)}, bf16[4,64,512]{2,1,0:T(8,128)(2,1)S(1)}, u32[]{:S(2)}, u32[]{:S(2)}) collective-permute-start(bf16[4,64,512]{2,1,0:T(8,128)(2,1)S(1)} %get-tuple-element.127), channel_id=1, source_target_pairs={{0,6},{1,7},{2,4},{3,5},{4,2},{5,3},{6,0},{7,1},{8,14},{9,15},{10,... | collective-permute-start | bytes 786440 | tf_op jit(solution)/shard_map/ppermute | solution.py:619
  214.4 13.5 %collective-permute-start.58 = (bf16[4,64,512]{2,1,0:T(8,128)(2,1)S(1)}, bf16[4,64,512]{2,1,0:T(8,128)(2,1)S(1)}, u32[]{:S(2)}, u32[]{:S(2)}) collective-permute-start(bf16[4,64,512]{2,1,0:T(8,128)(2,1)S(1)} %get-tuple-element.128), channel_id=1, source_target_pairs={{0,4},{1,5},{2,6},{3,7},{4,0},{5,1},{6,2},{7,3},{8,12},{9,13},{10,... | collective-permute-start | bytes 786440 | tf_op jit(solution)/shard_map/ppermute | solution.py:619
  (59 other events, 471.0 us)

commit v2 on v1

v2 whole, which is shorter than its diff:
```python
import functools
import math

import jax
import jax.numpy as jnp
from jax import lax
from jax.experimental import pallas as pl
from jax.experimental.pallas import tpu as pltpu
from jax.sharding import PartitionSpec as P

AXES = ("dp", "fsdp")
HEADS = 8
EPS = 1e-05
SCALE = 0.125
EXP_SCALE = SCALE * math.log2(math.e)
HIDE = -(2.0**60)
MIB = 2**20

BF = jnp.bfloat16
F32 = jnp.float32
NN = (((1,), (0,)), ((), ()))
NT = (((1,), (1,)), ((), ()))
TN = (((0,), (0,)), ((), ()))


def dot(a, b, dims=NN):
    return lax.dot_general(a, b, dims, preferred_element_type=F32)


def vmem():
    return pl.BlockSpec(memory_space=pltpu.VMEM)


def smem():
    return pl.BlockSpec(memory_space=pltpu.SMEM)


def shape(dims, dtype):
    return jax.ShapeDtypeStruct(dims, dtype)


def cost(us):
    return pl.CostEstimate(flops=int(us * 1.1e9), bytes_accessed=0, transcendentals=0)


def slots():
    return [(c, j, i) for c in range(2) for j in range(4) for i in range(4)]


def block_row(me, c, j, i, rows):
    return pl.multiple_of((me ^ (c | (j << 1) | (i << 3))) * rows, rows)


def row_stats(rows_in):
    mean = jnp.mean(rows_in, axis=-1, keepdims=True)
    centred = rows_in - mean
    spread = jnp.mean(centred * centred, axis=-1, keepdims=True)
    return centred, lax.rsqrt(spread + EPS)


def split_three(row):
    first = row.astype(BF).astype(F32)
    rest = row - first
    second = rest.astype(BF).astype(F32)
    return first, second, rest - second


def pack_kernel(qkv, mix, up, down, gain, shift, qv, proj, up_bias, a0, b0, b1, rows128):
    for pair in range(4):
        for part in range(3):
            base = 384 * pair + 128 * part
            a0[:, base : base + 128] = qkv[:, 512 * part + 128 * pair : 512 * part + 128 * pair + 128]
    rows128[...] = jnp.zeros_like(rows128)
    for index, ref in enumerate((gain, shift, qv, proj)):
        rows128[2 * index : 2 * index + 2, :] = ref[...].astype(F32)
    eye = (
        lax.broadcasted_iota(jnp.int32, (16, 16), 0) == lax.broadcasted_iota(jnp.int32, (16, 16), 1)
    ).astype(F32)
    columns = dot(eye.astype(BF), rows128[...].astype(BF), NT)
    bias = jnp.concatenate([jnp.zeros((1, 64), F32), up_bias[...].astype(F32)], axis=1)
    row = lax.broadcasted_iota(jnp.int32, (16, 128), 0)
    lane = lax.broadcasted_iota(jnp.int32, (16, 128), 1)
    a0[:, 1536:1664] = jnp.where((row == 0) & (lane >= 64), bias, columns).astype(BF)
    b0[:, 0:512] = mix[...]
    b0[:, 512:2560] = up[...]
    for part in range(4):
        b1[:, 512 * part : 512 * part + 512] = down[16 * part : 16 * part + 16, :]


def pack(qkv, mix, up, down, gain, shift, qv, proj, up_bias):
    return pl.pallas_call(
        pack_kernel,
        in_specs=[vmem()] * 9,
        out_specs=[vmem()] * 3,
        out_shape=[
            shape((16, 1664), BF),
            shape((16, 2560), BF),
            shape((16, 2048), BF),
        ],
        scratch_shapes=[pltpu.VMEM((128, 16), F32)],
        cost_estimate=cost(1.5),
        name="pack",
    )(qkv, mix, up, down, gain, shift, qv, proj, up_bias.reshape(1, 64))


def aux_rows(chain):
    row = lax.broadcasted_iota(jnp.int32, (128, chain.shape[1]), 0)
    low_bits = jnp.where(row < 7, (chain >> jnp.minimum(row, 6)) & 1, 0)
    high_bits = jnp.where(
        (row >= 7) & (row < 14), 1 - ((chain >> jnp.minimum(jnp.maximum(row - 7, 0), 6)) & 1), 0
    )
    bits = low_bits + high_bits
    query_side = bits.astype(F32) * HIDE
    key_side = jnp.where(row < 14, 1 - bits, jnp.where(row < 17, 1, 0)).astype(F32)
    return query_side.astype(BF), key_side.T.astype(BF)


def pair_forward(normed, weight, bias_q, bias_v, key_aux, qa, ot, outs, pair, block):
    q_out, k_out, v_out, o_out, ot_out, lse_out = outs
    rows = normed.shape[0]
    cols = slice(128 * pair, 128 * pair + 128)
    q2 = (dot(normed, weight[:, 0:128]) + bias_q).astype(BF)
    k2 = dot(normed, weight[:, 128:256]).astype(BF)
    v2 = (dot(normed, weight[:, 256:384]) + bias_v).astype(BF)
    q_out[:, cols] = q2
    k_out[:, cols] = k2
    v_out[:, cols] = v2
    qa[0:128, :] = q2.T
    vt = v2.T
    ones = (lax.broadcasted_iota(jnp.int32, (16, rows), 0) == 0).astype(F32).astype(BF)
    lane = lax.broadcasted_iota(jnp.int32, k2.shape, 1)
    zero = jnp.zeros_like(k2)
    keys = [
        jnp.concatenate([jnp.where((lane >= 64) == bool(h), k2, zero), key_aux], axis=1)
        for h in range(2)
    ]
    vts = [jnp.concatenate([vt[64 * h : 64 * h + 64], ones], axis=0) for h in range(2)]
    count = rows // block

    def score(index):
        q_cols = qa[:, block * index : block * index + block]
        return [dot(keys[h], q_cols) for h in range(2)]

    ahead = score(0)
    for index in range(count):
        scores = ahead
        if index + 1 < count:
            ahead = score(index + 1)
        span = slice(block * index, block * index + block)
        for h in range(2):
            peak = jnp.max(scores[h], axis=0, keepdims=True)
            probs = jnp.exp2((scores[h] - peak) * EXP_SCALE).astype(BF)
            mixed = dot(vts[h], probs)
            total = mixed[64:65]
            ot[64 * h : 64 * h + 64, span] = mixed[:64] * (1.0 / total)
            lse_out[2 * pair + h : 2 * pair + h + 1, span] = peak + jnp.log(total) * (1.0 / SCALE)
    ot_out[128 * pair : 128 * pair + 128, :] = ot[...].astype(BF)
    o_out[:, cols] = ot[...].T.astype(BF)


def forward_kernel(
    me_ref, tokens, chain, mine, other,
    q_out, k_out, v_out, o_out, ot_out, lse_out, weight, normed_out, normed_t, smalls, up_row,
    key_aux_out, query_aux_out, qa, ot, columns,
):
    me = me_ref[0]
    for c, j, i in slots():
        source = (mine, other)[c]
        row = block_row(me, c, j, i, 16)
        weight[pl.ds(row, 16), :] = source[4 * j + i, :, 0:1536]
        columns[pl.ds(row, 16), :] = source[4 * j + i, :, 1536:1664].astype(F32)
    smalls[...] = columns[...].T[0:8, :]
    lane = lax.broadcasted_iota(jnp.int32, (1, 128), 1)
    for a in range(16):
        even = pltpu.roll(columns[32 * a : 32 * a + 8, :], 64, 1)[0:1, :]
        odd = columns[32 * a + 16 : 32 * a + 17, :]
        up_row[:, 128 * a : 128 * a + 128] = jnp.where(lane < 64, even, odd)
    query_side, key_side = aux_rows(chain[...])
    qa[128:256, :] = query_side
    query_aux_out[...] = query_side
    key_aux_out[...] = key_side

    def norm_block(index, carry):
        span = pl.ds(pl.multiple_of(index * 256, 256), 256)
        centred, scale = row_stats(tokens[span, :].astype(F32))
        normed_out[span, :] = (centred * scale * smalls[0:1, :] + smalls[2:3, :]).astype(BF)
        return carry

    lax.fori_loop(0, tokens.shape[0] // 256, norm_block, 0)
    normed = normed_out[...]
    normed_t[0:512, :] = normed.T
    ones_row = lax.broadcasted_iota(jnp.int32, (16, normed.shape[0]), 0) == 0
    normed_t[512:528, :] = ones_row.astype(F32).astype(BF)
    outs = (q_out, k_out, v_out, o_out, ot_out, lse_out)
    for pair in range(4):
        cols = slice(128 * pair, 128 * pair + 128)
        pair_forward(
            normed, weight[:, 384 * pair : 384 * pair + 384], smalls[4:5, cols], smalls[5:6, cols],
            key_side, qa, ot, outs, pair, 512,
        )


def forward(me, tokens, chain, mine, other):
    rows = tokens.shape[0]
    return pl.pallas_call(
        forward_kernel,
        in_specs=[smem()] + [vmem()] * 4,
        out_specs=[vmem()] * 13,
        out_shape=[shape((rows, 512), BF)] * 4
        + [
            shape((512, rows), BF),
            shape((8, rows), F32),
            shape((512, 1536), BF),
            shape((rows, 512), BF),
            shape((528, rows), BF),
            shape((8, 512), F32),
            shape((1, 2048), F32),
            shape((rows, 128), BF),
            shape((128, rows), BF),
        ],
        scratch_shapes=[
            pltpu.VMEM((256, rows), BF),
            pltpu.VMEM((128, rows), F32),
            pltpu.VMEM((512, 128), F32),
        ],
        compiler_params=pltpu.CompilerParams(vmem_limit_bytes=40 * MIB),
        cost_estimate=cost(15),
        name="attend",
    )(me, tokens, chain, mine, other)


def gelu_parts(u):
    half_cdf = 0.5 + 0.5 * lax.erf(u * math.sqrt(0.5))
    density = jnp.exp2(u * u * (-0.5 * math.log2(math.e))) * (1.0 / math.sqrt(2.0 * math.pi))
    return u * half_cdf, half_cdf + u * density


def scatter_blocks(me, source, rows, base_block, blocks, send, keep, span):
    core = me & 1
    for half in range(blocks // 2):
        first = base_block + 2 * half
        row = 2 * half * rows
        r = (me ^ first) >> 1
        place = ((r & 3) << 2) | (r >> 2)
        kept = source[pl.ds(pl.multiple_of(row + core * rows, rows), rows), :]
        sent = source[pl.ds(pl.multiple_of(row + (1 - core) * rows, rows), rows), :]
        keep[place, :, span] = kept
        send[place, :, span] = sent.astype(BF)


def feed_first_kernel(
    me_ref, tokens, o_in, mine_a, other_a, mine_b, other_b, smalls, up_row, cot,
    output, middle, normed_t, grad_pre_out, d_send, d_keep, mix, up, down, normed, total, stage,
):
    me = me_ref[0]
    for c, j, i in slots():
        first, second = ((mine_a, mine_b), (other_a, other_b))[c]
        row = block_row(me, c, j, i, 16)
        mix[pl.ds(row, 16), :] = first[4 * j + i, :, 0:512]
        up[pl.ds(row, 16), :] = first[4 * j + i, :, 512:2560]
        for part in range(4):
            row4 = pl.multiple_of(block_row(me, c, j, i, 64) + 16 * part, 16)
            down[pl.ds(row4, 16), :] = second[4 * i + j, :, 512 * part : 512 * part + 512]
    rows = tokens.shape[0]
    block = 256

    def ahead(index, carry):
        span = pl.ds(pl.multiple_of(index * block, block), block)
        mid = tokens[span, :].astype(F32) + dot(o_in[span, :], mix[...]) + smalls[6:7, :]
        middle[span, :] = mid
        centred, scale = row_stats(mid)
        normed[span, :] = (centred * scale * smalls[1:2, :] + smalls[3:4, :]).astype(BF)
        total[span, :] = mid + smalls[7:8, :]
        return carry

    lax.fori_loop(0, rows // block, ahead, 0)
    normed_t[0:512, :] = normed[...].T
    ones_row = lax.broadcasted_iota(jnp.int32, (16, rows), 0) == 0
    normed_t[512:528, :] = ones_row.astype(F32).astype(BF)
    width = 512
    for chunk in range(2048 // width):
        span = slice(chunk * width, chunk * width + width)
        down_part = down[span, :]
        act, slope = gelu_parts(dot(normed[...], up[:, span]) + up_row[:, span])
        act_low = act.astype(BF)
        grad_pre_out[:, span] = (dot(cot[...], down_part, NT) * slope).astype(BF)
        total[...] += dot(act_low, down_part)
        stage[...] = dot(act_low, cot[...], TN)
        scatter_blocks(me, stage, 64, chunk * width // 64, width // 64, d_send, d_keep, slice(None))
    output[...] = total[...].astype(BF)


def feed_first(me, tokens, o_in, a_pair, b_pair, smalls, up_row, cot):
    rows = tokens.shape[0]
    return pl.pallas_call(
        feed_first_kernel,
        in_specs=[smem()] + [vmem()] * 9,
        out_specs=[vmem()] * 8,
        out_shape=[
            shape((rows, 512), BF),
            shape((rows, 512), F32),
            shape((528, rows), BF),
            shape((rows, 2048), BF),
            shape((16, 64, 512), BF),
            shape((16, 64, 512), F32),
            shape((512, 512), BF),
            shape((512, 2048), BF),
        ],
        scratch_shapes=[
            pltpu.VMEM((2048, 512), BF),
            pltpu.VMEM((rows, 512), BF),
            pltpu.VMEM((rows, 512), F32),
            pltpu.VMEM((512, 512), F32),
        ],
        compiler_params=pltpu.CompilerParams(vmem_limit_bytes=48 * MIB),
        cost_estimate=cost(18),
        name="feed_first",
    )(me, tokens, o_in, *a_pair, *b_pair, smalls, up_row, cot)


def feed_second_kernel(
    me_ref, middle, normed_t, grad_pre, mix, up, smalls, cot, ot_in,
    grad_middle, grad_att, m_send, m_keep, small_grads, up_bias_grad, low_rows, stage,
):
    me = me_ref[0]
    rows = middle.shape[0]
    block = 256
    width = 512
    for chunk in range(2048 // width):
        span = slice(chunk * width, chunk * width + width)
        stage[...] = dot(normed_t[...], grad_pre[:, span])
        up_bias_grad[:, span] = stage[512:513, :]
        scatter_blocks(me, stage, 16, 0, 32, m_send, m_keep, span)

    def behind(index, carry):
        gain_sum, shift_sum, branch_sum, cot_sum = carry
        span = pl.ds(pl.multiple_of(index * block, block), block)
        centred, scale = row_stats(middle[span, :])
        xh = centred * scale
        h = dot(grad_pre[span, :], up[...], NT)
        hg = h * smalls[1:2, :]
        cot_rows = cot[span, :].astype(F32)
        grad = cot_rows + scale * (
            hg
            - jnp.mean(hg, axis=-1, keepdims=True)
            - xh * jnp.mean(hg * xh, axis=-1, keepdims=True)
        )
        grad_middle[span, :] = grad
        low = grad.astype(BF)
        low_rows[span, :] = low
        grad_att[span, :] = dot(low, mix[...], NT).astype(BF)
        return (
            gain_sum + jnp.sum(h * xh, axis=0, keepdims=True),
            shift_sum + jnp.sum(h, axis=0, keepdims=True),
            branch_sum + jnp.sum(low.astype(F32), axis=0, keepdims=True),
            cot_sum + jnp.sum(cot_rows, axis=0, keepdims=True),
        )

    zero = jnp.zeros((1, 512), F32)
    sums = lax.fori_loop(0, rows // block, behind, (zero, zero, zero, zero))
    for index in range(4):
        small_grads[index : index + 1, :] = sums[index]
    small_grads[4:8, :] = jnp.zeros((4, 512), F32)
    stage[0:512, :] = dot(ot_in[...], low_rows[...])
    scatter_blocks(me, stage, 16, 0, 32, m_send, m_keep, slice(2048, 2560))


def feed_second(me, middle, normed_t, grad_pre, mix, up, smalls, cot, ot_in):
    rows = middle.shape[0]
    return pl.pallas_call(
        feed_second_kernel,
        in_specs=[smem()] + [vmem()] * 8,
        out_specs=[vmem()] * 6,
        out_shape=[
            shape((rows, 512), F32),
            shape((rows, 512), BF),
            shape((16, 16, 2560), BF),
            shape((16, 16, 2560), F32),
            shape((8, 512), F32),
            shape((1, 2048), F32),
        ],
        scratch_shapes=[pltpu.VMEM((rows, 512), BF), pltpu.VMEM((528, 512), F32)],
        compiler_params=pltpu.CompilerParams(vmem_limit_bytes=48 * MIB),
        cost_estimate=cost(11),
        name="feed_second",
    )(me, middle, normed_t, grad_pre, mix, up, smalls, cot, ot_in)


def pair_backward(q, k, v, do, ot_in, lse, key_aux, qa, da, dqt, acc_k, acc_v, gm, pair, block):
    k2 = k[...]
    v2 = v[...]
    rows = k2.shape[0]
    kt = k2.T
    lane = lax.broadcasted_iota(jnp.int32, k2.shape, 1)
    zero = jnp.zeros_like(k2)
    keys = []
    vals = []
    for h in range(2):
        own = (lane >= 64) == bool(h)
        keys.append(jnp.concatenate([jnp.where(own, k2, zero), key_aux], axis=1))
        vals.append(jnp.concatenate([jnp.where(own, v2, zero), key_aux], axis=1))
    qt = q[...].T
    dt = do[...].T
    product = dt.astype(F32) * ot_in[...].astype(F32)
    row = lax.broadcasted_iota(jnp.int32, (16, rows), 0)
    for h in range(2):
        qa[h, 0:128, :] = qt
        da[h, 0:128, :] = dt
        delta = jnp.sum(product[64 * h : 64 * h + 64], axis=0, keepdims=True)
        base = qa[h, 128:144, :].astype(F32)
        one, two, three = split_three(-lse[2 * pair + h : 2 * pair + h + 1, :])
        base = jnp.where(row == 14, one, jnp.where(row == 15, two, base))
        qa[h, 128:144, :] = base.astype(BF)
        qa[h, 144:160, :] = jnp.where(row == 0, three, 0.0).astype(BF)
        one, two, three = split_three(-delta)
        base = jnp.where(row == 14, one, jnp.where(row == 15, two, 0.0))
        da[h, 128:144, :] = base.astype(BF)
        da[h, 144:160, :] = jnp.where(row == 0, three, 0.0).astype(BF)
    small_lane = lax.broadcasted_iota(jnp.int32, (block, 128), 1)
    for index in range(rows // block):
        span = slice(block * index, block * index + block)
        do_rows = do[span, :]
        q_rows = q[span, :]
        blank = jnp.zeros_like(do_rows)
        sum_k = None
        sum_v = None
        for h in range(2):
            own = (small_lane >= 64) == bool(h)
            probs = jnp.exp2(dot(keys[h], qa[h, :, span]) * EXP_SCALE)
            grad = (probs * dot(vals[h], da[h, :, span])).astype(BF)
            probs = probs.astype(BF)
            dqt[64 * h : 64 * h + 64, span] = dot(kt[64 * h : 64 * h + 64, :], grad)
            part_k = dot(grad, jnp.where(own, q_rows, blank))
            part_v = dot(probs, jnp.where(own, do_rows, blank))
            sum_k = part_k if sum_k is None else sum_k + part_k
            sum_v = part_v if sum_v is None else sum_v + part_v
        if index == 0:
            acc_k[...] = sum_k
            acc_v[...] = sum_v
        else:
            acc_k[...] += sum_k
            acc_v[...] += sum_v
    gm[:, 0:128] = (dqt[...].T * SCALE).astype(BF)
    gm[:, 128:256] = (acc_k[...] * SCALE).astype(BF)
    gm[:, 256:384] = acc_v[...].astype(BF)


def backward_pair(q, k, v, do, ot_in, lse, key_aux, query_aux, gm, scratch, pair):
    qa, da, dqt, acc_k, acc_v = scratch
    for h in range(2):
        qa[h, 128:256, :] = query_aux[...]
        da[h, 128:256, :] = jnp.zeros((128, da.shape[2]), BF)
    pair_backward(q, k, v, do, ot_in, lse, key_aux[...], qa, da, dqt, acc_k, acc_v, gm, pair, 256)


def weight_terms(me, gm_first, gm, normed_t, weight, smalls, stage, send, keep, sums, vectors):
    stage[:, 0:384] = dot(normed_t[...], gm_first[...])
    stage[:, 384:768] = dot(normed_t[...], gm[...])
    total = stage[512:513, :]
    sums[0:1, :] = total
    scatter_blocks(me, stage, 16, 0, 32, send, keep, slice(0, 768))
    wide = weight[...].astype(F32)
    vectors[:, 0:1] = jnp.sum(stage[0:512, :] * wide, axis=1, keepdims=True)
    vectors[:, 1:2] = jnp.sum(wide * total, axis=1, keepdims=True)


def backward_even_kernel(pair, q, k, v, do, ot_in, lse, key_aux, query_aux, gm, *scratch):
    backward_pair(q, k, v, do, ot_in, lse, key_aux, query_aux, gm, scratch, pair)


def backward_odd_kernel(
    me_ref, q, k, v, do, ot_in, lse, key_aux, query_aux, gm_first, normed_t, weight, smalls,
    gm, send, keep, sums, vectors, *scratch,
):
    backward_pair(q, k, v, do, ot_in, lse, key_aux, query_aux, gm, scratch[:5], 1)
    weight_terms(
        me_ref[0], gm_first, gm, normed_t, weight, smalls, scratch[5], send, keep, sums, vectors
    )


def backward_last_kernel(
    me_ref, q, k, v, do, ot_in, lse, key_aux, query_aux, gm_first, normed_t, weight, smalls,
    small_grads, up_bias_grad, sums_first, vectors_first,
    gm, send, keep, *scratch,
):
    me = me_ref[0]
    stage, sums, vectors, columns = scratch[5:]
    backward_pair(q, k, v, do, ot_in, lse, key_aux, query_aux, gm, scratch[:5], 3)
    weight_terms(me, gm_first, gm, normed_t, weight, smalls, stage, send, keep, sums, vectors)
    columns[...] = jnp.zeros_like(columns)
    columns[1:2, :] = small_grads[0:1, :]
    columns[3:4, :] = small_grads[1:2, :]
    for pair in range(4):
        source = (sums_first, sums)[pair // 2]
        base = (pair % 2) * 384
        span = slice(128 * pair, 128 * pair + 128)
        columns[4:5, span] = source[0:1, base : base + 128]
        columns[5:6, span] = source[0:1, base + 256 : base + 384]
    columns[6:7, :] = small_grads[2:3, :]
    columns[7:8, :] = small_grads[3:4, :]
    columns[8:9, :] = smalls[0:1, :]
    columns[9:10, :] = smalls[2:3, :]
    tile = columns[...].T
    product = vectors[:, 0:1] + vectors_first[:, 0:1]
    plain = vectors[:, 1:2] + vectors_first[:, 1:2]
    gain_sum = (product - tile[:, 9:10] * plain) / tile[:, 8:9]
    lanes = lax.broadcasted_iota(jnp.int32, (512, 128), 1)
    stage[0:512, 0:128] = jnp.where(lanes == 0, gain_sum, jnp.where(lanes == 2, plain, tile))
    lane = lax.broadcasted_iota(jnp.int32, (1, 128), 1)
    for a in range(16):
        piece = up_bias_grad[:, 128 * a : 128 * a + 128]
        rolled = pltpu.roll(jnp.broadcast_to(piece, (8, 128)), 64, 1)[0:1, :]
        for half, values in enumerate((rolled, piece)):
            row = 32 * a + 16 * half
            stage[row : row + 1, 0:128] = jnp.where(lane < 64, stage[row : row + 1, 0:128], values)
    core = me & 1
    for half in range(16):
        r = (me ^ (2 * half)) >> 1
        place = ((r & 3) << 2) | (r >> 2)
        kept = pl.multiple_of(32 * half + core * 16, 16)
        sent = pl.multiple_of(32 * half + (1 - core) * 16, 16)
        keep[place, :, 768:896] = stage[pl.ds(kept, 16), 0:128]
        send[place, :, 768:896] = stage[pl.ds(sent, 16), 0:128].astype(BF)


def backward_scratch(rows):
    return [
        pltpu.VMEM((2, 256, rows), BF),
        pltpu.VMEM((2, 256, rows), BF),
        pltpu.VMEM((128, rows), F32),
        pltpu.VMEM((rows, 128), F32),
        pltpu.VMEM((rows, 128), F32),
    ]


def pair_specs(rows, pair):
    column = pl.BlockSpec((rows, 128), lambda i: (0, pair))
    return [column] * 4 + [
        pl.BlockSpec((128, rows), lambda i: (pair, 0)),
        vmem(), vmem(), vmem(),
    ]


def backward_even(pair, *operands):
    rows = operands[0].shape[0]
    return pl.pallas_call(
        functools.partial(backward_even_kernel, pair),
        grid=(1,),
        in_specs=pair_specs(rows, pair),
        out_specs=vmem(),
        out_shape=shape((rows, 384), BF),
        scratch_shapes=backward_scratch(rows),
        compiler_params=pltpu.CompilerParams(vmem_limit_bytes=32 * MIB),
        cost_estimate=cost(8),
        name=f"attend_back_{pair}",
    )(*operands)


def backward_odd(me, *operands):
    rows = operands[0].shape[0]
    return pl.pallas_call(
        backward_odd_kernel,
        grid=(1,),
        in_specs=[smem()]
        + pair_specs(rows, 1)
        + [vmem(), vmem(), pl.BlockSpec((512, 768), lambda i: (0, 0)), vmem()],
        out_specs=[vmem()] * 5,
        out_shape=[
            shape((rows, 384), BF),
            shape((16, 16, 768), BF),
            shape((16, 16, 768), F32),
            shape((8, 768), F32),
            shape((512, 128), F32),
        ],
        scratch_shapes=backward_scratch(rows) + [pltpu.VMEM((528, 768), F32)],
        compiler_params=pltpu.CompilerParams(vmem_limit_bytes=40 * MIB),
        cost_estimate=cost(9),
        name="attend_back_1",
    )(me, *operands)


def backward_last(me, *operands):
    rows = operands[0].shape[0]
    return pl.pallas_call(
        backward_last_kernel,
        grid=(1,),
        in_specs=[smem()]
        + pair_specs(rows, 3)
        + [vmem(), vmem(), pl.BlockSpec((512, 768), lambda i: (0, 1))]
        + [vmem()] * 5,
        out_specs=[vmem()] * 3,
        out_shape=[
            shape((rows, 384), BF),
            shape((16, 16, 896), BF),
            shape((16, 16, 896), F32),
        ],
        scratch_shapes=backward_scratch(rows)
        + [
            pltpu.VMEM((528, 768), F32),
            pltpu.VMEM((8, 768), F32),
            pltpu.VMEM((512, 128), F32),
            pltpu.VMEM((128, 512), F32),
        ],
        compiler_params=pltpu.CompilerParams(vmem_limit_bytes=40 * MIB),
        cost_estimate=cost(9),
        name="attend_back_3",
    )(me, *operands)


def input_kernel(tokens, gm0, gm1, gm2, gm3, weight, smalls, grad_middle, input_grad):
    block = 256

    def behind(index, carry):
        span = pl.ds(pl.multiple_of(index * block, block), block)
        centred, scale = row_stats(tokens[span, :].astype(F32))
        xh = centred * scale
        gm = jnp.concatenate([ref[span, :] for ref in (gm0, gm1, gm2, gm3)], axis=1)
        hg = dot(gm, weight[...], NT) * smalls[0:1, :]
        input_grad[span, :] = grad_middle[span, :] + scale * (
            hg
            - jnp.mean(hg, axis=-1, keepdims=True)
            - xh * jnp.mean(hg * xh, axis=-1, keepdims=True)
        )
        return carry

    lax.fori_loop(0, tokens.shape[0] // block, behind, 0)


def input_terms(*operands):
    rows = operands[0].shape[0]
    return pl.pallas_call(
        input_kernel,
        in_specs=[vmem()] * 8,
        out_specs=vmem(),
        out_shape=shape((rows, 512), F32),
        compiler_params=pltpu.CompilerParams(vmem_limit_bytes=32 * MIB),
        cost_estimate=cost(5),
        name="input_terms",
    )(*operands)


def swap(value, mask, count):
    return lax.ppermute(value, AXES, [(d, d ^ mask) for d in range(count)])


Z_MASKS = (8, 16, 24)
PLANE_MASKS = (2, 4, 6)


def swaps(value, masks, count):
    return [swap(value, mask, count) for mask in masks]


def after(value, *tokens):
    return lax.optimization_barrier((value, tokens))[0]


def group(own, others):
    joined = jnp.stack([own] + others)
    return joined.reshape((-1,) + joined.shape[-2:])


def merge(own, received):
    for part in received:
        own = own + part.astype(F32)
    return own


def slices(total, rows, width):
    quarters = total.reshape((4, -1, rows, width))
    return quarters[0], [quarters[j].astype(BF) for j in range(1, 4)]


def pack_whole(qkv, mix, up, down, gain, shift, qv, proj, up_bias):
    pieces = []
    for pair in range(4):
        for part in range(3):
            base = 512 * part + 128 * pair
            pieces.append(qkv[:, base : base + 128])
    rows = jnp.concatenate([gain, shift, qv, proj], axis=0)
    tile = jnp.pad(rows.T, ((0, 0), (0, 120))).reshape(32, 16, 128)
    tile = tile.at[:, 0, 64:128].set(up_bias.reshape(32, 64))
    a0 = jnp.concatenate([jnp.concatenate(pieces, 1).reshape(32, 16, 1536), tile], axis=2)
    b0 = jnp.concatenate([mix, up], axis=1).reshape(32, 16, 2560)
    b1 = down.reshape(32, 4, 16, 512).swapaxes(1, 2).reshape(32, 16, 2048)
    return a0, b0, b1


def relative_halves(blocks):
    parts = blocks.reshape((4, 4, 2) + blocks.shape[1:])
    parts = parts.transpose((2, 1, 0) + tuple(range(3, parts.ndim)))
    return parts[0].reshape((16,) + blocks.shape[1:]), parts[1].reshape((16,) + blocks.shape[1:])


def whole_blocks(send, keep):
    parts = jnp.stack([keep, send.astype(F32)]).reshape((2, 4, 4) + keep.shape[1:])
    parts = parts.transpose((2, 1, 0) + tuple(range(3, parts.ndim)))
    return parts.reshape((32,) + keep.shape[1:])


def body(cubic, count, tokens, chain_ids, qkv, mix, up, down, gain, shift, qv, proj, up_bias, cot):
    params = (qkv, mix, up, down, gain, shift, qv, proj, up_bias)
    if cubic:
        index = lax.axis_index("dp") * (count // lax.axis_size("dp")) + lax.axis_index("fsdp")
        me = index.astype(jnp.int32).reshape(1)
        a_own, b_own, c_own = pack(*params)
        a_recv = swaps(a_own, Z_MASKS, count)
        c_recv = swaps(c_own, PLANE_MASKS, count)
        a_col = group(a_own, a_recv)
        a_recv = swaps(a_col, PLANE_MASKS, count)
        b_recv = swaps(after(b_own, a_col), Z_MASKS, count)
        c_plane = group(c_own, [after(part, a_col) for part in c_recv])
        c_recv = swaps(c_plane, Z_MASKS, count)
        a_mine = group(a_col, a_recv)
        a_other = swap(a_mine, 1, count)
        b_col = group(b_own, [after(part, a_mine) for part in b_recv])
        b_recv = swaps(b_col, PLANE_MASKS, count)
        a_mine, a_other = after((a_mine, a_other), b_col)
    else:
        me = jnp.zeros((1,), jnp.int32)
        dims = (0, 0, 0, 0, 1, 1, 1, 1, 0)
        whole = [
            lax.all_gather(value, AXES, axis=dim, tiled=True)
            for value, dim in zip(params, dims, strict=True)
        ]
        a_parts, b_parts, c_parts = pack_whole(*whole)
        a_mine, a_other = relative_halves(a_parts)
        b_pair = relative_halves(b_parts)
        c_pair = [
            half.reshape(4, 4, 16, 2048).swapaxes(0, 1).reshape(16, 16, 2048)
            for half in relative_halves(c_parts)
        ]
    q, k, v, o, ot, lse, weight, normed, normed_t, smalls, up_row, key_aux, query_aux = forward(
        me, tokens, chain_ids, a_mine, a_other
    )
    if cubic:
        b_mine = group(b_col, [after(part, smalls) for part in b_recv])
        c_mine = group(c_plane, [after(part, smalls) for part in c_recv])
        b_pair = (b_mine, swap(b_mine, 1, count))
        c_pair = (c_mine, swap(c_mine, 1, count))
    output, middle, normed_two_t, grad_pre, d_send, d_keep, mix_whole, up_whole = feed_first(
        me, tokens, o, b_pair, c_pair, smalls, up_row, cot
    )
    if cubic:
        d_recv = swap(d_send, 1, count)
    grad_middle, grad_att, m_send, m_keep, small_grads, up_bias_grad = feed_second(
        me, middle, normed_two_t, grad_pre, mix_whole, up_whole, smalls, cot, ot
    )
    if cubic:
        d_total = merge(d_keep, [after(d_recv, small_grads)])
        d_own, d_parts = slices(d_total, 64, 512)
        d_recv = [swap(part, mask, count) for part, mask in zip(d_parts, PLANE_MASKS, strict=True)]
        m_recv = swap(m_send, 1, count)
        lse = after(lse, d_parts)
    gm0 = backward_even(0, q, k, v, grad_att, ot, lse, key_aux, query_aux)
    if cubic:
        m_total = merge(m_keep, [after(m_recv, gm0)])
        m_own, m_parts = slices(m_total, 16, 2560)
        m_recv = [swap(part, mask, count) for part, mask in zip(m_parts, PLANE_MASKS, strict=True)]
        lse = after(lse, m_parts)
    gm1, f_send, f_keep, sums, vectors = backward_odd(
        me, q, k, v, grad_att, ot, lse, key_aux, query_aux, gm0, normed_t, weight, smalls
    )
    if cubic:
        f_recv = swap(f_send, 1, count)
        d_total = merge(d_own, [after(part, sums) for part in d_recv])
        d_own, d_parts = slices(d_total, 64, 512)
        d_recv = [swap(part, mask, count) for part, mask in zip(d_parts, Z_MASKS, strict=True)]
        lse = after(lse, d_parts)
    gm2 = backward_even(2, q, k, v, grad_att, ot, lse, key_aux, query_aux)
    if cubic:
        m_total = merge(m_own, [after(part, gm2) for part in m_recv])
        m_own, m_parts = slices(m_total, 16, 2560)
        m_recv = [swap(part, mask, count) for part, mask in zip(m_parts, Z_MASKS, strict=True)]
        f_total = merge(f_keep, [after(f_recv, gm2)])
        f_own, f_parts = slices(f_total, 16, 768)
        f_recv = [swap(part, mask, count) for part, mask in zip(f_parts, PLANE_MASKS, strict=True)]
        down_grad = merge(d_own, [after(part, gm2) for part in d_recv])
        lse = after(lse, m_parts, f_parts)
    gm3, g_send, g_keep = backward_last(
        me, q, k, v, grad_att, ot, lse, key_aux, query_aux, gm2, normed_t, weight, smalls,
        small_grads, up_bias_grad, sums, vectors,
    )
    if cubic:
        g_total = merge(g_keep, [swap(g_send, 1, count)])
        g_own, g_parts = slices(g_total, 16, 896)
        g_recv = [swap(part, mask, count) for part, mask in zip(g_parts, PLANE_MASKS, strict=True)]
        smalls = after(smalls, g_parts)
    input_grad = input_terms(tokens, gm0, gm1, gm2, gm3, weight, smalls, grad_middle)
    if cubic:
        token = input_grad
        m_grad = merge(m_own, [after(part, g_parts) for part in m_recv])[0]
        f_total = merge(f_own, [after(part, g_parts) for part in f_recv])
        g_total = merge(g_own, [after(part, token) for part in g_recv])
        total = jnp.concatenate([f_total, g_total], axis=-1)
        own, parts = slices(total, 16, 1664)
        recv = [swap(part, mask, count) for part, mask in zip(parts, Z_MASKS, strict=True)]
        final = merge(own, recv)[0]
        m_grad = m_grad.reshape(16, 2560)
        final = final.reshape(16, 1664)
        down_grad = down_grad.reshape(64, 512)
        tile = final[:, 1536:1664]
        return (
            output, input_grad, unpack_columns([final[:, :768], final[:, 768:1536]]),
            m_grad[:, 2048:], m_grad[:, :2048], down_grad,
            tile[:, 0:2].T, tile[:, 2:4].T, tile[:, 4:6].T, tile[:, 6:8].T, tile[0, 64:128],
        )
    pairs = ((d_send, d_keep), (m_send, m_keep), (f_send, f_keep), (g_send, g_keep))
    blocks = [whole_blocks(s, r) for s, r in pairs]
    tiles = blocks[3][:, :, 768:896]
    joined = blocks[1].reshape(512, 2560)
    wholes = (
        blocks[0].reshape(2048, 512),
        joined[:, :2048],
        joined[:, 2048:],
        unpack_columns([blocks[2].reshape(512, 768), blocks[3][:, :, :768].reshape(512, 768)]),
        tiles[:, 0, 64:128].reshape(2048),
    )
    down_grad, up_grad, mix_grad, qkv_grad, bias_grad = [
        lax.psum_scatter(value, AXES, scatter_dimension=0, tiled=True) for value in wholes
    ]
    vectors = lax.psum_scatter(
        tiles[:, :, 0:8].reshape(512, 8).T, AXES, scatter_dimension=1, tiled=True
    )
    return (
        output, input_grad, qkv_grad, mix_grad, up_grad, down_grad,
        vectors[0:2], vectors[2:4], vectors[4:6], vectors[6:8], bias_grad,
    )


def unpack_columns(halves):
    pieces = []
    for part in range(3):
        for pair in range(4):
            base = (pair % 2) * 384 + 128 * part
            pieces.append(halves[pair // 2][:, base : base + 128])
    return jnp.concatenate(pieces, axis=1)


def solution(mesh):
    count = mesh.shape["dp"] * mesh.shape["fsdp"]
    cubic = count == 32

    def entry(*operands):
        return body(cubic, count, *operands)

    rows = P(AXES, None)
    columns = P(None, AXES)
    flat = P(AXES)
    return jax.shard_map(
        entry,
        mesh=mesh,
        in_specs=(rows,) * 6 + (columns,) * 4 + (flat, rows),
        out_specs=(rows,) * 6 + (columns,) * 4 + (flat,),
        check_vma=False,
    )
```

time: 241 us -> 199 us (0.83)
  starting transfers between devices: 75.1 us -> 53.1 us
  waiting for transfers between devices: 59 us -> 43.5 us
  other arithmetic: 11.5 us -> 4.85 us
  local copies, waits for them, and re-layouts: 7.72 us -> 10.2 us
    ppermute x63 -> x46, starting transfers between devices: 75.1 us -> 53.1 us  [swap(): return lax.ppermute(value, AXES, [(d, d ^ mask) for d in range(count)])]
    ppermute x63 -> x46, waiting for transfers between devices: 59 us -> 43.5 us  [swap(): return lax.ppermute(value, AXES, [(d, d ^ mask) for d in range(count)])]
    another operation x18 -> x13, other arithmetic: 9.48 us -> 3.99 us
    pallas_call x6 -> x9, Pallas kernels: 82.8 us -> 83.4 us  [the longest x1 20.3 us: feed_first(): pl.pallas_call(feed_first_kernel, in_specs=[smem()] + [vmem()] * 9, out_s...]
  transfers between devices with their start and end apart: 63 -> 46, of which waited for: 31 -> 19; matrix products, arithmetic and copies ran while one was open for 6% -> 3% of each run, Pallas kernels for 22% -> 27%
where the time goes in v2:
time: 199 us; the launch traced here: 197 us
  Pallas kernels  83.4 us (42%)
  starting transfers between devices  53.1 us (27%)
  waiting for transfers between devices  43.5 us (22%)
  local copies, waits for them, and re-layouts  10.2 us (5%)
  other arithmetic  4.85 us (2%)
    ppermute x46, starting transfers between devices, swap(): return lax.ppermute(value, AXES, [(d, d ^ mask) for d in range(count)])  53.1 us
    ppermute x46, waiting for transfers between devices, swap(): return lax.ppermute(value, AXES, [(d, d ^ mask) for d in range(count)])  43.5 us
    pallas_call x1, Pallas kernels, feed_first(): pl.pallas_call(feed_first_kernel, in_specs=[smem()] + [vmem()] * 9, out_s...  20.3 us
    pallas_call x1, Pallas kernels, forward(): pl.pallas_call(forward_kernel, in_specs=[smem()] + [vmem()] * 4, out_spec...  15.3 us
    pallas_call x1, Pallas kernels, feed_second(): pl.pallas_call(feed_second_kernel, in_specs=[smem()] + [vmem()] * 8, out_...  13.7 us
    pallas_call x2, Pallas kernels, backward_even(): pl.pallas_call(functools.partial(backward_even_kernel, pair), grid=(1,),...  12.1 us
    pallas_call x1, Pallas kernels, backward_last(): pl.pallas_call(backward_last_kernel, grid=(1,), in_specs=[smem()] + pair_...  8.3 us
    unnamed x55, local copies, waits for them, and re-layouts  8.04 us
  transfers between devices with their start and end apart: 46, of which 19 were waited for; matrix products, arithmetic and copies ran while one was open for 3% of the time, Pallas kernels for 27%

profile of v2, /device:TPU:0, one launch (start us, length us, event | category | flops | bytes accessed | tf_op | source)
XLA Modules:
  0.0 196.5 jit_solution(12314069677320238455)
XLA Ops:
  2.4 5.1 %collective-permute-start.2 = (bf16[16,1664]{1,0:T(8,128)(2,1)}, bf16[16,1664]{1,0:T(8,128)(2,1)S(1)}, u32[]{:S(2)}, u32[]{:S(2)}) collective-permute-start(bf16[16,1664]{1,0:T(8,128)(2,1)} %get-tuple-element.89), channel_id=1, source_target_pairs={{0,24},{1,25},{2,26},{3,27},{4,28},{5,29},{6,30},{7,31},{8,16},{9,... | collective-permute-start | bytes 159752 | tf_op jit(solution)/shard_map/ppermute | solution.py:643
  10.1 2.7 %collective-permute-done.1 = bf16[16,1664]{1,0:T(8,128)(2,1)S(1)} collective-permute-done((bf16[16,1664]{1,0:T(8,128)(2,1)}, bf16[16,1664]{1,0:T(8,128)(2,1)S(1)}, u32[]{:S(2)}, u32[]{:S(2)}) %collective-permute-start.1) | collective-permute-done | bytes 53280 | tf_op jit(solution)/shard_map/ppermute | solution.py:643
  13.6 2.5 %collective-permute-start.5 = (bf16[4,16,1664]{2,1,0:T(8,128)(2,1)S(1)}, bf16[4,16,1664]{2,1,0:T(8,128)(2,1)S(1)}, u32[]{:S(2)}, u32[]{:S(2)}) collective-permute-start(bf16[4,16,1664]{2,1,0:T(8,128)(2,1)S(1)} %get-tuple-element.216), channel_id=1, source_target_pairs={{0,6},{1,7},{2,4},{3,5},{4,2},{5,3},{6,0},{7,1},{8,14},{9,15},{10,... | collective-permute-start | bytes 638984 | tf_op jit(solution)/shard_map/ppermute | solution.py:643
  17.2 5.6 %collective-permute-done.5 = bf16[4,16,1664]{2,1,0:T(8,128)(2,1)S(1)} collective-permute-done((bf16[4,16,1664]{2,1,0:T(8,128)(2,1)S(1)}, bf16[4,16,1664]{2,1,0:T(8,128)(2,1)S(1)}, u32[]{:S(2)}, u32[]{:S(2)}) %collective-permute-start.5) | collective-permute-done | bytes 213024 | tf_op jit(solution)/shard_map/ppermute | solution.py:643
  22.8 2.5 %collective-permute-done.4 = bf16[4,16,1664]{2,1,0:T(8,128)(2,1)S(1)} collective-permute-done((bf16[4,16,1664]{2,1,0:T(8,128)(2,1)S(1)}, bf16[4,16,1664]{2,1,0:T(8,128)(2,1)S(1)}, u32[]{:S(2)}, u32[]{:S(2)}) %collective-permute-start.4) | collective-permute-done | bytes 213024 | tf_op jit(solution)/shard_map/ppermute | solution.py:643
  29.2 2.0 %collective-permute-start.9 = (bf16[16,2560]{1,0:T(8,128)(2,1)S(1)}, bf16[16,2560]{1,0:T(8,128)(2,1)S(1)}, u32[]{:S(2)}, u32[]{:S(2)}) collective-permute-start(bf16[16,2560]{1,0:T(8,128)(2,1)S(1)} %copy-done.16), channel_id=1, source_target_pairs={{0,24},{1,25},{2,26},{3,27},{4,28},{5,29},{6,30},{7,31},{8,16},{9,... | collective-permute-start | bytes 245768 | tf_op jit(solution)/shard_map/ppermute | solution.py:643
  36.3 2.5 %collective-permute-start.17 = (bf16[4,16,2048]{2,1,0:T(8,128)(2,1)S(1)}, bf16[4,16,2048]{2,1,0:T(8,128)(2,1)S(1)}, u32[]{:S(2)}, u32[]{:S(2)}) collective-permute-start(bf16[4,16,2048]{2,1,0:T(8,128)(2,1)S(1)} %get-tuple-element.211), channel_id=1, source_target_pairs={{0,8},{1,9},{2,10},{3,11},{4,12},{5,13},{6,14},{7,15},{8,0},{9,1},... | collective-permute-start | bytes 786440 | tf_op jit(solution)/shard_map/ppermute | solution.py:643
  38.8 5.8 %collective-permute-done.8 = bf16[16,2560]{1,0:T(8,128)(2,1)S(1)} collective-permute-done((bf16[16,2560]{1,0:T(8,128)(2,1)S(1)}, bf16[16,2560]{1,0:T(8,128)(2,1)S(1)}, u32[]{:S(2)}, u32[]{:S(2)}) %collective-permute-start.8) | collective-permute-done | bytes 81952 | tf_op jit(solution)/shard_map/ppermute | solution.py:643
  48.2 15.3 %attend.1 = (bf16[1024,512]{1,0:T(8,128)(2,1)S(1)}, bf16[1024,512]{1,0:T(8,128)(2,1)S(1)}, bf16[1024,512]{1,0:T(8,128)(2,1)S(1)}, bf16[1024,512]{1,0:T(8,128)(2,...) custom-call(s32[1]{0:T(128)} %bitcast.me_ref, ...), custom_call_target="tpu_custom_call" | custom-call | flops 16499999744 | tf_op jit(solution)/shard_map/attend/pallas_call | solution.py:205
  63.6 2.1 %collective-permute-start.19 = (bf16[4,16,2048]{2,1,0:T(8,128)(2,1)S(1)}, bf16[4,16,2048]{2,1,0:T(8,128)(2,1)S(1)}, u32[]{:S(2)}, u32[]{:S(2)}) collective-permute-start(bf16[4,16,2048]{2,1,0:T(8,128)(2,1)S(1)} %get-tuple-element.211), channel_id=1, source_target_pairs={{0,24},{1,25},{2,26},{3,27},{4,28},{5,29},{6,30},{7,31},{8,16},{9,... | collective-permute-start | bytes 786440 | tf_op jit(solution)/shard_map/ppermute | solution.py:643
  66.0 6.0 %collective-permute-done.19 = bf16[4,16,2048]{2,1,0:T(8,128)(2,1)S(1)} collective-permute-done((bf16[4,16,2048]{2,1,0:T(8,128)(2,1)S(1)}, bf16[4,16,2048]{2,1,0:T(8,128)(2,1)S(1)}, u32[]{:S(2)}, u32[]{:S(2)}) %collective-permute-start.19) | collective-permute-done | bytes 262176 | tf_op jit(solution)/shard_map/ppermute | solution.py:643
  72.2 2.6 %collective-permute-done.20.other_b = bf16[16,16,2048]{2,1,0:T(8,128)(2,1)S(1)} collective-permute-done((bf16[16,16,2048]{2,1,0:T(8,128)(2,1)S(1)}, bf16[16,16,2048]{2,1,0:T(8,128)(2,1)S(1)}, u32[]{:S(2)}, u32[]{:S(2)}) %collective-permute-start.20) | collective-permute-done | bytes 1048608 | tf_op jit(solution)/shard_map/ppermute | solution.py:643
  75.9 20.3 %feed_first.1 = (bf16[1024,512]{1,0:T(8,128)(2,1)}, f32[1024,512]{1,0:T(8,128)}, bf16[528,1024]{1,0:T(8,128)(2,1)}, bf16[1024,2048]{1,0:T(8,128)(2,1)}, bf16[16,...) custom-call(s32[1]{0:T(128)} %bitcast.me_ref, ...), custom_call_target="tpu_custom_call" | custom-call | flops 19800000512 | tf_op jit(solution)/shard_map/feed_first/pallas_call | solution.py:295
  97.6 13.7 %feed_second.1 = (f32[1024,512]{1,0:T(8,128)}, bf16[1024,512]{1,0:T(8,128)(2,1)S(1)}, bf16[16,16,2560]{2,1,0:T(8,128)(2,1)S(1)}, f32[16,16,2560]{2,1,0:T(8,128)}...) custom-call(s32[1]{0:T(128)} %bitcast.me_ref, f32[1024,512]{1,0:T(8,128)} %get-tuple-element.114.middle, ...), custom_call_target="tpu_custom_call" | custom-call | flops 12099999744 | tf_op jit(solution)/shard_map/feed_second/pallas_call | solution.py:370
  117.0 6.0 %attend_back_0.1.gm_first.gm0 = bf16[1024,384]{1,0:T(8,128)(2,1)S(1)} custom-call(bf16[1024,512]{1,0:T(8,128)(2,1)S(1)} %get-tuple-element.111.q, bf16[1024,512]{1,0:T(8,128)(2,1)S(1)} %get-tuple-element.112.k, bf16[1024,512]{1,0:T(8,128)(2,1)S(1)} %copy-done.5, bf16[1024,512]{1,0:T(8,128)(2,1)S(1)} %get-tuple-element.120.do, ...), custom_call_target="tpu_custom_call" | custom-call | flops 8800000000 | tf_op jit(solution)/shard_map/attend_back_0/pallas_call | solution.py:546
  126.7 7.8 %attend_back_1.1 = (bf16[1024,384]{1,0:T(8,128)(2,1)S(1)}, bf16[16,16,768]{2,1,0:T(8,128)(2,1)S(1)}, f32[16,16,768]{2,1,0:T(8,128)S(1)}, f32[8,768]{1,0:T(8,128)S(1)}, f32[512,128]{1,0:T(8,128)S(1)}) custom-call(s32[1]{0:T(128)} %bitcast.me_ref, bf16[1024,512]{1,0:T(8,128)(2,1)S(1)} %get-tuple-element.111.q, bf16[1024,512]{1,0:T(8,128)(2,1)S(1)} %get-tuple-element.112.k, ...), custom_call_target="tpu_custom_call" | custom-call | flops 9900000256 | tf_op jit(solution)/shard_map/attend_back_1/pallas_call | solution.py:561
  135.2 6.0 %attend_back_2.1.gm_first.gm2 = bf16[1024,384]{1,0:T(8,128)(2,1)S(1)} custom-call(bf16[1024,512]{1,0:T(8,128)(2,1)S(1)} %get-tuple-element.111.q, bf16[1024,512]{1,0:T(8,128)(2,1)S(1)} %get-tuple-element.112.k, bf16[1024,512]{1,0:T(8,128)(2,1)S(1)} %copy-done.5, bf16[1024,512]{1,0:T(8,128)(2,1)S(1)} %get-tuple-element.120.do, ...), custom_call_target="tpu_custom_call" | custom-call | flops 8800000000 | tf_op jit(solution)/shard_map/attend_back_2/pallas_call | solution.py:546
  144.5 8.3 %attend_back_3.1 = (bf16[1024,384]{1,0:T(8,128)(2,1)S(1)}, bf16[16,16,896]{2,1,0:T(8,128)(2,1)S(1)}, f32[16,16,896]{2,1,0:T(8,128)S(1)}) custom-call(s32[1]{0:T(128)} %bitcast.me_ref, bf16[1024,512]{1,0:T(8,128)(2,1)S(1)} %get-tuple-element.111.q, bf16[1024,512]{1,0:T(8,128)(2,1)S(1)} %get-tuple-element.112.k, bf16[1024,512]{1,0:T(8,128)(2,1)S(1)} %copy-done.5, ...), custom_call_target="tpu_custom_call" | custom-call | flops 9900000256 | tf_op jit(solution)/shard_map/attend_back_3/pallas_call | solution.py:584
  152.9 2.0 %collective-permute-start.45 = (bf16[1,64,512]{2,1,0:T(8,128)(2,1)S(1)}, bf16[1,64,512]{2,1,0:T(8,128)(2,1)S(1)}, u32[]{:S(2)}, u32[]{:S(2)}) collective-permute-start(bf16[1,64,512]{2,1,0:T(8,128)(2,1)S(1)} %get-tuple-element.207), channel_id=1, source_target_pairs={{0,24},{1,25},{2,26},{3,27},{4,28},{5,29},{6,30},{7,31},{8,16},{9,... | collective-permute-start | bytes 196616 | tf_op jit(solution)/shard_map/ppermute | solution.py:643
  157.3 2.0 collective-permute-done.45
  159.3 4.1 %collective-permute-done.44 = bf16[1,64,512]{2,1,0:T(8,128)(2,1)S(1)} collective-permute-done((bf16[1,64,512]{2,1,0:T(8,128)(2,1)S(1)}, bf16[1,64,512]{2,1,0:T(8,128)(2,1)S(1)}, u32[]{:S(2)}, u32[]{:S(2)}) %collective-permute-start.44) | collective-permute-done | bytes 65568 | tf_op jit(solution)/shard_map/ppermute | solution.py:643
  171.0 4.2 %input_terms.1 = f32[1024,512]{1,0:T(8,128)} custom-call(bf16[1024,512]{1,0:T(8,128)(2,1)S(1)} %copy-done.1, bf16[1024,384]{1,0:T(8,128)(2,1)S(1)} %attend_back_0.1.gm_first.gm0, bf16[1024,384]{1,0:T(8,128)(2,1)S(1)} %get-tuple-element.135.gm1, bf16[1024,384]{1,0:T(8,128)(2,1)S(1)} %attend_back_2.1.gm_first.gm2, ...), custom_call_target="tpu_custom_call" | custom-call | flops 5500000256 | tf_op jit(solution)/shard_map/input_terms/pallas_call | solution.py:631
  175.2 2.5 %collective-permute-start.40 = (bf16[1,16,2560]{2,1,0:T(8,128)(2,1)S(1)}, bf16[1,16,2560]{2,1,0:T(8,128)(2,1)S(1)}, u32[]{:S(2)}, u32[]{:S(2)}) collective-permute-start(bf16[1,16,2560]{2,1,0:T(8,128)(2,1)S(1)} %get-tuple-element.204), channel_id=1, source_target_pairs={{0,8},{1,9},{2,10},{3,11},{4,12},{5,13},{6,14},{7,15},{8,0},{9,1},... | collective-permute-start | bytes 245768 | tf_op jit(solution)/shard_map/ppermute | solution.py:643
  181.3 2.3 %collective-permute-done.36 = bf16[4,16,896]{2,1,0:T(8,128)(2,1)S(1)} collective-permute-done((bf16[4,16,896]{2,1,0:T(8,128)(2,1)S(1)}, bf16[4,16,896]{2,1,0:T(8,128)(2,1)S(1)}, u32[]{:S(2)}, u32[]{:S(2)}) %collective-permute-start.36) | collective-permute-done | bytes 114720 | tf_op jit(solution)/shard_map/ppermute | solution.py:643
  (162 shorter events, 61.1 us)
Async XLA Ops:
  13.6 9.2 %collective-permute-start.5 = (bf16[4,16,1664]{2,1,0:T(8,128)(2,1)S(1)}, bf16[4,16,1664]{2,1,0:T(8,128)(2,1)S(1)}, u32[]{:S(2)}, u32[]{:S(2)}) collective-permute-start(bf16[4,16,1664]{2,1,0:T(8,128)(2,1)S(1)} %get-tuple-element.216), channel_id=1, source_target_pairs={{0,6},{1,7},{2,4},{3,5},{4,2},{5,3},{6,0},{7,1},{8,14},{9,15},{10,... | collective-permute-start | bytes 638984 | tf_op jit(solution)/shard_map/ppermute | solution.py:643
  16.1 9.2 %collective-permute-start.4 = (bf16[4,16,1664]{2,1,0:T(8,128)(2,1)S(1)}, bf16[4,16,1664]{2,1,0:T(8,128)(2,1)S(1)}, u32[]{:S(2)}, u32[]{:S(2)}) collective-permute-start(bf16[4,16,1664]{2,1,0:T(8,128)(2,1)S(1)} %get-tuple-element.216), channel_id=1, source_target_pairs={{0,4},{1,5},{2,6},{3,7},{4,0},{5,1},{6,2},{7,3},{8,12},{9,13},{10,... | collective-permute-start | bytes 638984 | tf_op jit(solution)/shard_map/ppermute | solution.py:643
  25.5 21.4 %collective-permute-start.6 = (bf16[16,16,1664]{2,1,0:T(8,128)(2,1)S(1)}, bf16[16,16,1664]{2,1,0:T(8,128)(2,1)S(1)}, u32[]{:S(2)}, u32[]{:S(2)}) collective-permute-start(bf16[16,16,1664]{2,1,0:T(8,128)(2,1)S(1)} %bitcast.50), channel_id=1, source_target_pairs={{0,1},{1,0},{2,3},{3,2},{4,5},{5,4},{6,7},{7,6},{8,9},{9,8},{10,11... | collective-permute-start | bytes 2555912 | tf_op jit(solution)/shard_map/ppermute | solution.py:643
  31.2 13.5 %collective-permute-start.8 = (bf16[16,2560]{1,0:T(8,128)(2,1)S(1)}, bf16[16,2560]{1,0:T(8,128)(2,1)S(1)}, u32[]{:S(2)}, u32[]{:S(2)}) collective-permute-start(bf16[16,2560]{1,0:T(8,128)(2,1)S(1)} %copy-done.16), channel_id=1, source_target_pairs={{0,16},{1,17},{2,18},{3,19},{4,20},{5,21},{6,22},{7,23},{8,24},{9,... | collective-permute-start | bytes 245768 | tf_op jit(solution)/shard_map/ppermute | solution.py:643
  31.7 12.9 %collective-permute-start.7 = (bf16[16,2560]{1,0:T(8,128)(2,1)S(1)}, bf16[16,2560]{1,0:T(8,128)(2,1)S(1)}, u32[]{:S(2)}, u32[]{:S(2)}) collective-permute-start(bf16[16,2560]{1,0:T(8,128)(2,1)S(1)} %copy-done.16), channel_id=1, source_target_pairs={{0,8},{1,9},{2,10},{3,11},{4,12},{5,13},{6,14},{7,15},{8,0},{9,1},... | collective-permute-start | bytes 245768 | tf_op jit(solution)/shard_map/ppermute | solution.py:643
  33.6 38.4 %collective-permute-start.18 = (bf16[4,16,2048]{2,1,0:T(8,128)(2,1)S(1)}, bf16[4,16,2048]{2,1,0:T(8,128)(2,1)S(1)}, u32[]{:S(2)}, u32[]{:S(2)}) collective-permute-start(bf16[4,16,2048]{2,1,0:T(8,128)(2,1)S(1)} %get-tuple-element.211), channel_id=1, source_target_pairs={{0,16},{1,17},{2,18},{3,19},{4,20},{5,21},{6,22},{7,23},{8,24},{9,... | collective-permute-start | bytes 786440 | tf_op jit(solution)/shard_map/ppermute | solution.py:643
  36.3 35.7 %collective-permute-start.17 = (bf16[4,16,2048]{2,1,0:T(8,128)(2,1)S(1)}, bf16[4,16,2048]{2,1,0:T(8,128)(2,1)S(1)}, u32[]{:S(2)}, u32[]{:S(2)}) collective-permute-start(bf16[4,16,2048]{2,1,0:T(8,128)(2,1)S(1)} %get-tuple-element.211), channel_id=1, source_target_pairs={{0,8},{1,9},{2,10},{3,11},{4,12},{5,13},{6,14},{7,15},{8,0},{9,1},... | collective-permute-start | bytes 786440 | tf_op jit(solution)/shard_map/ppermute | solution.py:643
  44.7 21.0 %collective-permute-start.11 = (bf16[4,16,2560]{2,1,0:T(8,128)(2,1)S(1)}, bf16[4,16,2560]{2,1,0:T(8,128)(2,1)S(1)}, u32[]{:S(2)}, u32[]{:S(2)}) collective-permute-start(bf16[4,16,2560]{2,1,0:T(8,128)(2,1)S(1)} %get-tuple-element.206), channel_id=1, source_target_pairs={{0,4},{1,5},{2,6},{3,7},{4,0},{5,1},{6,2},{7,3},{8,12},{9,13},{10,... | collective-permute-start | bytes 983048 | tf_op jit(solution)/shard_map/ppermute | solution.py:643
  46.2 19.5 %collective-permute-start.10 = (bf16[4,16,2560]{2,1,0:T(8,128)(2,1)S(1)}, bf16[4,16,2560]{2,1,0:T(8,128)(2,1)S(1)}, u32[]{:S(2)}, u32[]{:S(2)}) collective-permute-start(bf16[4,16,2560]{2,1,0:T(8,128)(2,1)S(1)} %get-tuple-element.206), channel_id=1, source_target_pairs={{0,2},{1,3},{2,0},{3,1},{4,6},{5,7},{6,4},{7,5},{8,10},{9,11},{10,... | collective-permute-start | bytes 983048 | tf_op jit(solution)/shard_map/ppermute | solution.py:643
  47.0 16.7 %collective-permute-start.12 = (bf16[4,16,2560]{2,1,0:T(8,128)(2,1)S(1)}, bf16[4,16,2560]{2,1,0:T(8,128)(2,1)S(1)}, u32[]{:S(2)}, u32[]{:S(2)}) collective-permute-start(bf16[4,16,2560]{2,1,0:T(8,128)(2,1)S(1)} %get-tuple-element.206), channel_id=1, source_target_pairs={{0,6},{1,7},{2,4},{3,5},{4,2},{5,3},{6,0},{7,1},{8,14},{9,15},{10,... | collective-permute-start | bytes 983048 | tf_op jit(solution)/shard_map/ppermute | solution.py:643
  65.9 9.0 %collective-permute-start.13 = (bf16[16,16,2560]{2,1,0:T(8,128)(2,1)S(1)}, bf16[16,16,2560]{2,1,0:T(8,128)(2,1)S(1)}, u32[]{:S(2)}, u32[]{:S(2)}) collective-permute-start(bf16[16,16,2560]{2,1,0:T(8,128)(2,1)S(1)} %bitcast.52), channel_id=1, source_target_pairs={{0,1},{1,0},{2,3},{3,2},{4,5},{5,4},{6,7},{7,6},{8,9},{9,8},{10,11... | collective-permute-start | bytes 3932168 | tf_op jit(solution)/shard_map/ppermute | solution.py:643
  96.3 15.5 %collective-permute-start.21 = (bf16[16,64,512]{2,1,0:T(8,128)(2,1)S(1)}, bf16[16,64,512]{2,1,0:T(8,128)(2,1)}, u32[]{:S(2)}, u32[]{:S(2)}) collective-permute-start(bf16[16,64,512]{2,1,0:T(8,128)(2,1)S(1)} %get-tuple-element.123), channel_id=1, source_target_pairs={{0,1},{1,0},{2,3},{3,2},{4,5},{5,4},{6,7},{7,6},{8,9},{9,8},{10,11... | collective-permute-start | bytes 3145736 | tf_op jit(solution)/shard_map/ppermute | solution.py:643
  111.3 11.7 %collective-permute-start.22 = (bf16[16,16,2560]{2,1,0:T(8,128)(2,1)S(1)}, bf16[16,16,2560]{2,1,0:T(8,128)(2,1)S(1)}, u32[]{:S(2)}, u32[]{:S(2)}) collective-permute-start(bf16[16,16,2560]{2,1,0:T(8,128)(2,1)S(1)} %get-tuple-element.130), channel_id=1, source_target_pairs={{0,1},{1,0},{2,3},{3,2},{4,5},{5,4},{6,7},{7,6},{8,9},{9,8},{10,11... | collective-permute-start | bytes 3932168 | tf_op jit(solution)/shard_map/ppermute | solution.py:643
  113.4 21.0 %collective-permute-start.25 = (bf16[4,64,512]{2,1,0:T(8,128)(2,1)S(1)}, bf16[4,64,512]{2,1,0:T(8,128)(2,1)S(1)}, u32[]{:S(2)}, u32[]{:S(2)}) collective-permute-start(bf16[4,64,512]{2,1,0:T(8,128)(2,1)S(1)} %get-tuple-element.193), channel_id=1, source_target_pairs={{0,6},{1,7},{2,4},{3,5},{4,2},{5,3},{6,0},{7,1},{8,14},{9,15},{10,... | collective-permute-start | bytes 786440 | tf_op jit(solution)/shard_map/ppermute | solution.py:643
  115.2 19.9 %collective-permute-start.24 = (bf16[4,64,512]{2,1,0:T(8,128)(2,1)S(1)}, bf16[4,64,512]{2,1,0:T(8,128)(2,1)S(1)}, u32[]{:S(2)}, u32[]{:S(2)}) collective-permute-start(bf16[4,64,512]{2,1,0:T(8,128)(2,1)S(1)} %get-tuple-element.194), channel_id=1, source_target_pairs={{0,4},{1,5},{2,6},{3,7},{4,0},{5,1},{6,2},{7,3},{8,12},{9,13},{10,... | collective-permute-start | bytes 786440 | tf_op jit(solution)/shard_map/ppermute | solution.py:643
  116.5 18.6 %collective-permute-start.23 = (bf16[4,64,512]{2,1,0:T(8,128)(2,1)S(1)}, bf16[4,64,512]{2,1,0:T(8,128)(2,1)S(1)}, u32[]{:S(2)}, u32[]{:S(2)}) collective-permute-start(bf16[4,64,512]{2,1,0:T(8,128)(2,1)S(1)} %get-tuple-element.195), channel_id=1, source_target_pairs={{0,2},{1,3},{2,0},{3,1},{4,6},{5,7},{6,4},{7,5},{8,10},{9,11},{10,... | collective-permute-start | bytes 786440 | tf_op jit(solution)/shard_map/ppermute | solution.py:643
  123.6 17.6 %collective-permute-start.28 = (bf16[4,16,2560]{2,1,0:T(8,128)(2,1)S(1)}, bf16[4,16,2560]{2,1,0:T(8,128)(2,1)S(1)}, u32[]{:S(2)}, u32[]{:S(2)}) collective-permute-start(bf16[4,16,2560]{2,1,0:T(8,128)(2,1)S(1)} %get-tuple-element.190), channel_id=1, source_target_pairs={{0,6},{1,7},{2,4},{3,5},{4,2},{5,3},{6,0},{7,1},{8,14},{9,15},{10,... | collective-permute-start | bytes 983048 | tf_op jit(solution)/shard_map/ppermute | solution.py:643
  125.4 17.3 %collective-permute-start.27 = (bf16[4,16,2560]{2,1,0:T(8,128)(2,1)S(1)}, bf16[4,16,2560]{2,1,0:T(8,128)(2,1)S(1)}, u32[]{:S(2)}, u32[]{:S(2)}) collective-permute-start(bf16[4,16,2560]{2,1,0:T(8,128)(2,1)S(1)} %get-tuple-element.191), channel_id=1, source_target_pairs={{0,4},{1,5},{2,6},{3,7},{4,0},{5,1},{6,2},{7,3},{8,12},{9,13},{10,... | collective-permute-start | bytes 983048 | tf_op jit(solution)/shard_map/ppermute | solution.py:643
  152.8 15.7 %collective-permute-start.30 = (bf16[16,16,896]{2,1,0:T(8,128)(2,1)S(1)}, bf16[16,16,896]{2,1,0:T(8,128)(2,1)S(1)}, u32[]{:S(2)}, u32[]{:S(2)}) collective-permute-start(bf16[16,16,896]{2,1,0:T(8,128)(2,1)S(1)} %get-tuple-element.152), channel_id=1, source_target_pairs={{0,1},{1,0},{2,3},{3,2},{4,5},{5,4},{6,7},{7,6},{8,9},{9,8},{10,11... | collective-permute-start | bytes 1376264 | tf_op jit(solution)/shard_map/ppermute | solution.py:643
  164.1 16.2 %collective-permute-start.42 = (bf16[1,16,2560]{2,1,0:T(8,128)(2,1)S(1)}, bf16[1,16,2560]{2,1,0:T(8,128)(2,1)S(1)}, u32[]{:S(2)}, u32[]{:S(2)}) collective-permute-start(bf16[1,16,2560]{2,1,0:T(8,128)(2,1)S(1)} %get-tuple-element.202), channel_id=1, source_target_pairs={{0,24},{1,25},{2,26},{3,27},{4,28},{5,29},{6,30},{7,31},{8,16},{9,... | collective-permute-start | bytes 245768 | tf_op jit(solution)/shard_map/ppermute | solution.py:643
  165.9 15.4 %collective-permute-start.41 = (bf16[1,16,2560]{2,1,0:T(8,128)(2,1)S(1)}, bf16[1,16,2560]{2,1,0:T(8,128)(2,1)S(1)}, u32[]{:S(2)}, u32[]{:S(2)}) collective-permute-start(bf16[1,16,2560]{2,1,0:T(8,128)(2,1)S(1)} %get-tuple-element.203), channel_id=1, source_target_pairs={{0,16},{1,17},{2,18},{3,19},{4,20},{5,21},{6,22},{7,23},{8,24},{9,... | collective-permute-start | bytes 245768 | tf_op jit(solution)/shard_map/ppermute | solution.py:643
  165.9 9.3 %collective-permute-start.33 = (bf16[4,16,768]{2,1,0:T(8,128)(2,1)S(1)}, bf16[4,16,768]{2,1,0:T(8,128)(2,1)S(1)}, u32[]{:S(2)}, u32[]{:S(2)}) collective-permute-start(bf16[4,16,768]{2,1,0:T(8,128)(2,1)S(1)} %get-tuple-element.199), channel_id=1, source_target_pairs={{0,6},{1,7},{2,4},{3,5},{4,2},{5,3},{6,0},{7,1},{8,14},{9,15},{10,... | collective-permute-start | bytes 294920 | tf_op jit(solution)/shard_map/ppermute | solution.py:643
  167.3 10.4 %collective-permute-start.32 = (bf16[4,16,768]{2,1,0:T(8,128)(2,1)S(1)}, bf16[4,16,768]{2,1,0:T(8,128)(2,1)S(1)}, u32[]{:S(2)}, u32[]{:S(2)}) collective-permute-start(bf16[4,16,768]{2,1,0:T(8,128)(2,1)S(1)} %get-tuple-element.200), channel_id=1, source_target_pairs={{0,4},{1,5},{2,6},{3,7},{4,0},{5,1},{6,2},{7,3},{8,12},{9,13},{10,... | collective-permute-start | bytes 294920 | tf_op jit(solution)/shard_map/ppermute | solution.py:643
  168.5 10.7 %collective-permute-start.31 = (bf16[4,16,768]{2,1,0:T(8,128)(2,1)S(1)}, bf16[4,16,768]{2,1,0:T(8,128)(2,1)S(1)}, u32[]{:S(2)}, u32[]{:S(2)}) collective-permute-start(bf16[4,16,768]{2,1,0:T(8,128)(2,1)S(1)} %get-tuple-element.201), channel_id=1, source_target_pairs={{0,2},{1,3},{2,0},{3,1},{4,6},{5,7},{6,4},{7,5},{8,10},{9,11},{10,... | collective-permute-start | bytes 294920 | tf_op jit(solution)/shard_map/ppermute | solution.py:643
  (42 other events, 365.4 us)
